TPU v7x, 32 devices: a whole 2x2x4 slice. The times are simulated.
32 devices in a mesh: dp: 8 (over z, x), fsdp: 4 (over y, core).
Axes of the slice: x: 2, y: 2, z: 4, core: 2. Of those that a mesh axis runs over, the one named last changes fastest.
Arguments:
- chars: int32 [64, 256], P(('dp', 'fsdp')), may hold values from 0 to 26
- steps: int32 [64], P(('dp', 'fsdp')), may hold values from 0 to 999
- embed: bfloat16 [13824], P(('dp', 'fsdp')), may hold values from -4 to 4
- layer_params: bfloat16 [2, 3216384], P(None, ('dp', 'fsdp')), may hold values from -2 to 2, as said below
- cotangent: bfloat16 [64, 256, 512], P(('dp', 'fsdp')), may hold values from -6 to 6
Outputs:
- out_act: bfloat16 [64, 256, 512], P(('dp', 'fsdp'))
- grad_embed: float32 [13824], P(('dp', 'fsdp'))
- grad_params: float32 [2, 3216384], P(None, ('dp', 'fsdp'))
Inputs may be any that keep to these rules, and one draw needn't show every extreme that they name: `layer_params`: parameters of 2 layers in the layout of the steps.
All inputs are finite; a program needn't handle non-finite values.
Results may differ from a plain program's by a relative error of at most 0.01.
Values may be sent and summed in bfloat16 or wider, within the bound.
No kernel may reach another device: no remote copies, remote signals or barrier semaphores. Data moves between devices by JAX's collectives and lax.ppermute only.
A program may use at most 256 MiB of HBM per device.

v0:
```python
import functools
import math

import jax
import jax.numpy as jnp
from jax import lax
from jax.experimental import pallas as pl
from jax.experimental.pallas import tpu as pltpu
from jax.sharding import PartitionSpec as P

D = 512
HEADS = 8
FF = 2048
VOCAB = 27
TD = 128
HD = 64
LANES = 128
EPSILON = 1e-05
AXES = ("dp", "fsdp")
F32 = jnp.float32
BF16 = jnp.bfloat16
VMEM_BYTES = 52 * 2**20

(
    N_CHARS, N_EMB, N_W_TIME, N_W_QKV, N_W_OUT, N_W_UP, N_W_DOWN,
    N_VECTORS, N_TABLE, N_X, N_A, N_QKV, N_PROB, N_O,
    N_X2, N_A2, N_GL, N_SLOPE, N_STREAM, N_OUTPUT, N_COTANGENT,
    N_GRAD, N_GRAD_IN, N_REST, N_KEEP, N_SEND, N_TABLE_OUT, N_EMB_T,
    N_CHUNKS, N_FLAT, N_FLAT_TABLE, N_CUTS, N_CUT_SEMS, N_NORMED, N_TOTAL,
    N_QKV_GRAD, N_HEADS_GRAD,
) = range(37)

ROW_GAIN_ONE, ROW_BIAS_ONE, ROW_W_TIME, ROW_B_TIME = 0, 4, 8, 520
ROW_QKV, ROW_OUT, ROW_GAIN_TWO, ROW_BIAS_TWO = 524, 6668, 8716, 8720
ROW_UP, ROW_B_UP, ROW_DOWN, ROW_B_DOWN, ROW_END = 8724, 16916, 16932, 25124, 25128
CHUNK_PAD = 832


def ceil_to(value, step):
    return -(-value // step) * step


class Geometry:
    def __init__(self, devices, shard, embed_shard):
        self.devices, self.shard, self.embed_shard = devices, shard, embed_shard
        self.param_rows = max(self.count(d, shard) for d in range(devices))
        self.embed_rows = max(self.count(d, embed_shard) for d in range(devices))
        self.embed_at = ceil_to(self.param_rows, 8)
        self.rows = ceil_to(max(self.embed_at + 8, self.param_rows + 2 * self.embed_rows), 16)

    @staticmethod
    def first(d, size):
        return d * size // LANES

    @staticmethod
    def count(d, size):
        return -(-(d + 1) * size // LANES) - d * size // LANES


def params(flops, nbytes, weight=0):
    flops, nbytes = max(flops * weight, 1000), max(nbytes * weight, 1000)
    return dict(
        compiler_params=pltpu.CompilerParams(vmem_limit_bytes=VMEM_BYTES),
        cost_estimate=pl.CostEstimate(flops=flops, bytes_accessed=nbytes, transcendentals=0),
    )


VM = pl.BlockSpec(memory_space=pltpu.VMEM)
SM = pl.BlockSpec(memory_space=pltpu.SMEM)
HBM = pl.BlockSpec(memory_space=pltpu.HBM)


def nn(left, right):
    return lax.dot_general(left, right, (((1,), (0,)), ((), ())), preferred_element_type=F32)


def nt(left, right):
    return lax.dot_general(left, right, (((1,), (1,)), ((), ())), preferred_element_type=F32)


def tn(left, right):
    return nn(left.T, right)


def shift_in(flat, offset):
    rolled = pltpu.roll(flat, offset, 1)
    above = jnp.concatenate([jnp.zeros((1, LANES), F32), rolled[:-1]], 0)
    lane = lax.broadcasted_iota(jnp.int32, flat.shape, 1)
    return jnp.where(lane >= offset, rolled, above)


def shift_out(flat, offset):
    rolled = pltpu.roll(flat, lax.rem(LANES - offset, LANES), 1)
    below = jnp.concatenate([rolled[1:], jnp.zeros((1, LANES), F32)], 0)
    lane = lax.broadcasted_iota(jnp.int32, flat.shape, 1)
    return jnp.where(lane < LANES - offset, rolled, below)


def pack_kernel(geo, place_ref, layers_ref, embed_ref, first_ref, second_ref):
    main = geo.embed_at
    for layer, out_ref in ((0, first_ref), (1, second_ref)):
        moved = shift_in(layers_ref[layer].astype(F32), place_ref[1])
        if layer == 0:
            tail = shift_in(embed_ref[...].astype(F32), place_ref[2])
            parts = [moved[:main], tail] + ([moved[main + 8 :]] if geo.rows > main + 8 else [])
            moved = jnp.concatenate(parts, 0)
        out_ref[...] = moved.astype(BF16)


def pack_shards(geo, place, layer_params, embed):
    layers = jnp.pad(layer_params, ((0, 0), (0, geo.rows * LANES - geo.shard)))
    table = jnp.pad(embed, (0, 8 * LANES - geo.embed_shard))
    out = jax.ShapeDtypeStruct((geo.rows, LANES), BF16)
    return pl.pallas_call(
        functools.partial(pack_kernel, geo),
        out_shape=(out, out),
        in_specs=[SM, VM, VM],
        out_specs=(VM, VM),
        **params(10**6, geo.rows * 1024),
    )(place, layers.reshape(2, geo.rows, LANES), table.reshape(8, LANES))


def finish_kernel(geo, fast, place_ref, *refs):
    grads_ref, embed_ref, moved = refs[-3:]
    parts = refs[:-3]
    count = 4 if fast else 1
    for layer in range(2):
        total = parts[layer * count][...].astype(F32)
        for part in parts[layer * count + 1 : (layer + 1) * count]:
            total = total + part[...].astype(F32)
        moved[pl.ds(layer * geo.rows, geo.rows), :] = shift_out(total, place_ref[1])
        if fast and layer == 0:
            first, size = geo.param_rows, geo.embed_rows
            lower, upper = total[first : first + size], total[first + size : first + 2 * size]
            tail = jnp.where(place_ref[3] >= 2, upper, lower)
            tail = jnp.concatenate([tail, jnp.zeros((8 - size, LANES), F32)], 0)
    if not fast:
        tail = parts[2][...]
    embed_ref[...] = shift_out(tail, place_ref[2])
    for r in range(ceil_to(geo.shard, LANES) // LANES):
        size = min(LANES, geo.shard - r * LANES)
        grads_ref[:, r * LANES : r * LANES + size] = moved[pl.ds(r, 2, stride=geo.rows), :][:, :size]


def finish(geo, fast, place, operands):
    grads, table = pl.pallas_call(
        functools.partial(finish_kernel, geo, fast),
        out_shape=(
            jax.ShapeDtypeStruct((2, geo.shard), F32),
            jax.ShapeDtypeStruct((8, LANES), F32),
        ),
        in_specs=[SM] + [VM] * len(operands),
        out_specs=(VM, VM),
        scratch_shapes=[pltpu.VMEM((2 * geo.rows, LANES), F32)],
        **params(10**6, geo.rows * 4096),
    )(place, *operands)
    return grads, table.reshape(-1)[: geo.embed_shard]


PARTS = {N_W_UP: (1, 4), N_W_DOWN: (0, 4), N_GL: (1, 4), N_SLOPE: (1, 4), N_PROB: (0, 2), N_QKV: (0, 2)}


def parts_of(name, parted):
    return range(PARTS[name][1]) if name in parted else range(1)


def part_of(ref, name, part, parted):
    if name not in parted:
        return ref
    dim, count = PARTS[name]
    size = ref.shape[dim] // count
    index = [slice(None)] * len(ref.shape)
    index[dim] = pl.ds(part * size, size)
    return ref.at[tuple(index)]


class Staged:
    def __init__(self, sources, targets, held, sems, parted):
        self.held, self.pending, self.sent, self.parted = held, {}, [], parted
        self.targets, self.sems = targets, sems
        order = sorted((part, place, name) for place, name in enumerate(sources) for part in parts_of(name, parted))
        for part, _, name in order:
            copy = pltpu.make_async_copy(
                part_of(sources[name], name, part, parted), part_of(held[name], name, part, parted), sems.at[len(self.pending)]
            )
            copy.start()
            self.pending[name, part] = copy
        self.used = len(order)

    def get(self, name, part=None):
        for one in parts_of(name, self.parted) if part is None or name not in self.parted else [part]:
            if (name, one) in self.pending:
                self.pending.pop((name, one)).wait()
        return self.held[name]

    def put(self, name, part=None):
        for one in parts_of(name, self.parted) if part is None else [part]:
            copy = pltpu.make_async_copy(
                part_of(self.held[name], name, one, self.parted), part_of(self.targets[name], name, one, self.parted), self.sems.at[self.used]
            )
            copy.start()
            self.used += 1
            self.sent.append(copy)

    def close(self):
        for copy in list(self.pending.values()) + self.sent:
            copy.wait()


def staged_call(kernel, place, operands, results, scratch, flops, raw=(), semaphores=0, unheld=(), parted=()):
    names, outs, temps = list(operands), list(results), list(scratch)

    held_outs = [name for name in outs if name not in unheld]

    def whole(place_ref, *refs):
        raws, refs = refs[: len(raw)], refs[len(raw) :]
        sources, refs = dict(zip(names, refs)), refs[len(names) :]
        targets, refs = dict(zip(outs, refs)), refs[len(outs) :]
        held, refs = dict(zip(names + held_outs, refs)), refs[len(names) + len(held_outs) :]
        extra, refs = dict(zip(temps, refs)), refs[len(temps) :]
        staged = Staged(sources, targets, held, refs[0], parted)
        kernel(place_ref, raws, staged, extra, refs[-1])
        staged.close()

    buffers = [pltpu.VMEM(v.shape, v.dtype) for v in (*operands.values(), *(results[name] for name in held_outs))]
    sems = [pltpu.SemaphoreType.DMA((sum(len(parts_of(name, parted)) for name in names + held_outs),))]
    if semaphores:
        sems.append(pltpu.SemaphoreType.DMA((semaphores,)))
    found = pl.pallas_call(
        whole,
        out_shape=tuple(results.values()),
        in_specs=[SM] + [HBM] * (len(raw) + len(names)),
        out_specs=(HBM,) * len(outs),
        scratch_shapes=buffers + list(scratch.values()) + sems,
        **params(flops, 2 * 10**7, 1),
    )(place, *raw, *operands.values())
    return dict(zip(outs, found))


def like(dtype, *shape):
    return jax.ShapeDtypeStruct(shape, dtype)


def unpack(geo, layer, plan, me, chunk_refs, held, flat, flat_table, out, sems):
    copies = []
    for source, pieces in zip(chunk_refs, plan):
        for src_at, relative, absolute, dst_at, count in pieces:
            if absolute is None:
                target = held.at[lax.bitwise_xor(me, relative), pl.ds(dst_at, count)]
                origin = source.at[pl.ds(src_at, count)]
            else:
                target, origin = held, source
            copies.append(pltpu.make_async_copy(origin, target, sems.at[len(copies)]))
    for copy in copies:
        copy.start()
    for copy in copies:
        copy.wait()
    for d in range(geo.devices):
        block = held[d].astype(F32)
        start, rows = geo.first(d, geo.shard), geo.count(d, geo.shard)
        split = (d * geo.shard) % LANES != 0
        if split:
            shared = flat[pl.ds(start, 1), :] + block[:1]
        flat[pl.ds(start, rows), :] = block[:rows]
        if split:
            flat[pl.ds(start, 1), :] = shared
        if layer == 0:
            tail = block[geo.embed_at : geo.embed_at + 8]
            start, rows = geo.first(d, geo.embed_shard), geo.count(d, geo.embed_shard)
            split = (d * geo.embed_shard) % LANES != 0
            if split:
                shared = flat_table[pl.ds(start, 1), :] + tail[:1]
            flat_table[pl.ds(start, rows), :] = tail[:rows]
            if split:
                flat_table[pl.ds(start, 1), :] = shared
    vectors = out[N_VECTORS]
    for row, start, width in (
        (0, ROW_GAIN_ONE, 4),
        (1, ROW_BIAS_ONE, 4),
        (2, ROW_B_TIME, 4),
        (3, ROW_GAIN_TWO, 4),
        (4, ROW_BIAS_TWO, 4),
        (5, ROW_B_DOWN, 4),
        (6, ROW_B_UP, 16),
    ):
        for c in range(width):
            vectors[row : row + 1, c * LANES : (c + 1) * LANES] = flat[pl.ds(start + c, 1), :]
    for name, start, rows, width in (
        (N_W_TIME, ROW_W_TIME, TD, 4),
        (N_W_QKV, ROW_QKV, D, 12),
        (N_W_OUT, ROW_OUT, D, 4),
        (N_W_UP, ROW_UP, D, 16),
        (N_W_DOWN, ROW_DOWN, FF, 4),
    ):
        for c in range(width):
            out[name][:, c * LANES : (c + 1) * LANES] = flat[pl.ds(start + c, rows, stride=width), :].astype(BF16)
    if layer == 0:
        table = out[N_TABLE]
        table[...] = jnp.zeros(table.shape, BF16)
        for c in range(4):
            table[0:VOCAB, c * LANES : (c + 1) * LANES] = flat_table[pl.ds(c, VOCAB, stride=4), :].astype(BF16)


WEIGHTS = {
    N_W_QKV: like(BF16, D, 3 * D),
    N_W_OUT: like(BF16, D, D),
    N_W_UP: like(BF16, D, FF),
    N_W_DOWN: like(BF16, FF, D),
    N_VECTORS: like(F32, 8, FF),
}


def unpack_scratch(geo, layer):
    scratch = {
        N_CHUNKS: pltpu.VMEM((geo.devices, geo.rows, LANES), BF16),
        N_FLAT: pltpu.VMEM((ROW_END + CHUNK_PAD, LANES), F32),
        N_FLAT_TABLE: pltpu.VMEM((4 * 32, LANES), F32),
        N_W_TIME: pltpu.VMEM((TD, D), BF16),
    }
    if layer == 0:
        scratch[N_TABLE] = pltpu.VMEM((32, D), BF16)
    return scratch


def split_gathered(gathered):
    plan = tuple(tuple(pieces) for array, pieces in gathered)
    return [array for array, pieces in gathered], plan, sum(len(pieces) for pieces in plan)


def norm_stats(values):
    mean = jnp.mean(values, -1, keepdims=True)
    centered = values - mean
    variance = jnp.mean(centered * centered, -1, keepdims=True)
    scale = lax.rsqrt(variance + EPSILON)
    return centered * scale, scale


ROW_BLOCK = 64


def norm_ahead(values, gain, bias, out):
    for r in range(0, values.shape[0], ROW_BLOCK):
        rows = slice(r, r + ROW_BLOCK)
        unit, _ = norm_stats(values[rows, :])
        out[rows, :] = (unit * gain + bias).astype(BF16)


def norm_back(grad, values, gain, passed, out):
    grad_gain, grad_bias = jnp.zeros((8, D), F32), jnp.zeros((8, D), F32)
    for r in range(0, values.shape[0], ROW_BLOCK):
        rows = slice(r, r + ROW_BLOCK)
        unit, scale = norm_stats(values[rows, :])
        block = grad[rows, :]
        grad_gain = grad_gain + jnp.sum((block * unit).reshape(-1, 8, D), 0)
        grad_bias = grad_bias + jnp.sum(block.reshape(-1, 8, D), 0)
        inner = block * gain
        shifted = inner - jnp.mean(inner, -1, keepdims=True)
        back = scale * (shifted - unit * jnp.mean(inner * unit, -1, keepdims=True))
        out[rows, :] = passed[rows, :].astype(F32) + back
    return jnp.sum(grad_gain, 0, keepdims=True), jnp.sum(grad_bias, 0, keepdims=True)


def gelu_both(u):
    root = math.sqrt(2.0 / math.pi)
    square = u * u
    t = jnp.tanh(root * (u + 0.044715 * (square * u)))
    half = 0.5 * (1.0 + t)
    slope = half + 0.5 * u * (1.0 - t * t) * (root * (1.0 + 3.0 * 0.044715 * square))
    return u * half, slope


def head_masks(shape, scale):
    lane = lax.broadcasted_iota(jnp.int32, shape, 1)
    one = jnp.where(lane < HD, scale, 0.0).astype(BF16)
    two = jnp.where(lane < HD, 0.0, scale).astype(BF16)
    return one, two


def ahead_attn(seqs, stream, emb, w_time, w_qkv, w_out, vectors, x, a, qkv, prob, o, x2, a2, done):
    tokens = x.shape[0]
    length = tokens // seqs
    time_vec = nn(emb[...], w_time[...]) + vectors[2:3, :D]
    for s in range(seqs):
        x[s * length : (s + 1) * length, :] = stream[s * length : (s + 1) * length] + time_vec[s : s + 1]
    done(N_X)
    norm_ahead(x, vectors[0:1, :D], vectors[1:2, :D], a)
    done(N_A)
    for c in range(3):
        part = slice(c * D, (c + 1) * D)
        qkv[:, part] = nn(a[...], w_qkv[:, part]).astype(BF16)
    done(N_QKV)
    masks = head_masks((length, LANES), 1.0 / math.sqrt(HD))
    heads = [(s, pair, h) for s in range(seqs) for pair in range(HEADS // 2) for h in range(2)]

    def cut(s, pair, c):
        return qkv[s * length : (s + 1) * length, c * D + pair * LANES : c * D + (pair + 1) * LANES]

    def scores_of(s, pair, h):
        return nt(cut(s, pair, 1) * masks[h], cut(s, pair, 0))

    ahead = [scores_of(*heads[i]) for i in range(4)]
    mixed = []
    for i, (s, pair, h) in enumerate(heads):
        scores = ahead.pop(0)
        if i + 4 < len(heads):
            ahead.append(scores_of(*heads[i + 4]))
        top = jnp.max(scores, 0, keepdims=True)
        expd = jnp.exp(scores - top)
        low = (expd * (1.0 / jnp.sum(expd, 0, keepdims=True))).astype(BF16)
        prob[s * HEADS + 2 * pair + h] = low
        v_t = cut(s, pair, 2).T
        mixed.append(nn(v_t[h * HD : (h + 1) * HD], low))
        if h == 1:
            rows = slice(s * length, (s + 1) * length)
            o[rows, pair * LANES : (pair + 1) * LANES] = jnp.concatenate(mixed, 0).T.astype(BF16)
            mixed = []
    done(N_PROB)
    done(N_O)
    x2[...] = x[...] + nn(o[...], w_out[...])
    done(N_X2)
    norm_ahead(x2, vectors[3:4, :D], vectors[4:5, :D], a2)
    done(N_A2)


def ahead_mlp(x2, a2, w_up, w_down, vectors, gl, slope, done):
    parts = [slice(c * D, (c + 1) * D) for c in range(FF // D)]

    def up(c):
        return nn(a2()[...], w_up(c)[:, parts[c]])

    total, u = None, up(0)
    for c, part in enumerate(parts):
        value, rate = gelu_both(u + vectors()[6:7, part])
        low = value.astype(BF16)
        gl[:, part] = low
        slope[:, part] = rate.astype(BF16)
        done(N_GL, c)
        done(N_SLOPE, c)
        if c + 1 < len(parts):
            u = up(c + 1)
        step = nn(low, w_down(c)[part, :])
        total = step if total is None else total + step
    return x2()[...] + vectors()[5:6, :D] + total


class Chunks:
    def __init__(self, geo, fast, me, held, targets, sems):
        self.geo, self.fast, self.me, self.held, self.targets, self.sems = geo, fast, me, held, targets, sems
        self.copies = []

    def cut(self, d, flat, base, table=None):
        geo, slot = self.geo, d % (self.geo.devices // 2)
        block = flat[pl.ds(geo.first(d, geo.shard) - base, geo.rows), :]
        if table is not None:
            first, size = geo.param_rows, geo.embed_rows
            tails = [
                table[pl.ds(geo.first(e, geo.embed_shard), size), :] for e in (d, d + geo.devices // 2)
            ]
            block = jnp.concatenate([block[:first], *tails, block[first + 2 * size :]], 0)
        self.held[slot] = block.astype(BF16)
        source, sem = self.held.at[slot], self.sems.at[slot]
        if not self.fast:
            self.copies.append(pltpu.make_async_copy(source, self.targets[0].at[slot], sem))
            self.copies[-1].start()
            return
        relative = lax.bitwise_xor(self.me, d)
        row = lax.bitwise_and(relative, 4) + lax.bitwise_and(relative, 2)
        row = row + lax.bitwise_and(lax.shift_right_logical(relative, 3), 1)
        keep, send = (pltpu.make_async_copy(source, target.at[row], sem) for target in self.targets)
        core = lax.bitwise_and(relative, 1)

        @pl.when(core == 0)
        def _():
            keep.start()

        @pl.when(core == 1)
        def _():
            send.start()

        self.copies.append(keep)

    def close(self):
        for copy in self.copies:
            copy.wait()


def back_mlp(geo, chunks, grad_in, x2, a2, gl, slope, w_up, w_down, vectors, grad, rest, flat, base, normed, done):
    grad_low = grad_in()[...].astype(BF16)
    flat[pl.ds(ROW_END - base, CHUNK_PAD), :] = jnp.zeros((CHUNK_PAD, LANES), F32)
    grad_bias = jnp.sum(grad_low.astype(F32), 0, keepdims=True)
    for c in range(4):
        flat[pl.ds(ROW_B_DOWN - base + c, 1), :] = grad_bias[:, c * LANES : (c + 1) * LANES]
    parts = [slice(j * D, (j + 1) * D) for j in range(FF // D)]

    def hidden_grad(j):
        return nt(grad_low, w_down(j)[parts[j], :])

    total, hidden = None, hidden_grad(0)
    for j, part in enumerate(parts):
        up_grad = (hidden * slope(j)[:, part].astype(F32)).astype(BF16)
        bias_grad = jnp.sum(up_grad.astype(F32), 0, keepdims=True)
        if j + 1 < len(parts):
            hidden = hidden_grad(j + 1)
        down = tn(gl(j)[:, part], grad_low)
        for c in range(4):
            cols = slice(c * LANES, (c + 1) * LANES)
            flat[pl.ds(ROW_B_UP - base + 4 * j + c, 1), :] = bias_grad[:, cols]
            flat[pl.ds(ROW_DOWN - base + 4 * D * j + c, D, stride=4), :] = down[:, cols]
        up = tn(a2()[...], up_grad)
        for c in range(4):
            cols = slice(c * LANES, (c + 1) * LANES)
            flat[pl.ds(ROW_UP - base + 4 * j + c, D, stride=16), :] = up[:, cols]
        step = nt(up_grad, w_up(j)[:, part])
        total = step if total is None else total + step
    normed[...] = total
    for d in range(geo.devices // 2, geo.devices):
        chunks.cut(d, flat, base)
    grad_gain, grad_bias = norm_back(normed, x2(), vectors()[3:4, :D], grad_in(), grad)
    done(N_GRAD)
    for c in range(4):
        cols = slice(c * LANES, (c + 1) * LANES)
        flat[pl.ds(ROW_GAIN_TWO - base + c, 1), :] = grad_gain[:, cols]
        flat[pl.ds(ROW_BIAS_TWO - base + c, 1), :] = grad_bias[:, cols]
    rest[...] = flat[pl.ds(ROW_GAIN_TWO - base, rest.shape[0]), :].astype(BF16)
    done(N_REST)


def back_attn(
    geo, seqs, chunks, table, embed_outs, grad_in, x, a, qkv, prob, o, w_qkv, w_out, vectors, emb_t, rest, total,
    flat, qkv_grad, heads_grad, normed, chars, done,
):
    tokens = normed.shape[0]
    length = tokens // seqs
    grad_low = grad_in()[...].astype(BF16)
    heads_grad[...] = nt(grad_low, w_out()[...]).astype(BF16)
    out_grad = tn(o()[...], grad_low)
    for c in range(4):
        flat[pl.ds(ROW_OUT + c, D, stride=4), :] = out_grad[:, c * LANES : (c + 1) * LANES]
    masks = head_masks((length, LANES), 1.0)
    scale = 1.0 / math.sqrt(HD)
    lane = lax.broadcasted_iota(jnp.int32, (length, LANES), 1)
    qkv, prob = qkv(), prob()
    heads = [(s, pair, h) for s in range(seqs) for pair in range(HEADS // 2) for h in range(2)]

    def cut(s, pair, c):
        return qkv[s * length : (s + 1) * length, c * D + pair * LANES : c * D + (pair + 1) * LANES]

    def go_of(s, pair):
        return heads_grad[s * length : (s + 1) * length, pair * LANES : (pair + 1) * LANES]

    def prob_grad_of(s, pair, h):
        return nt(cut(s, pair, 2) * masks[h], go_of(s, pair))

    ahead = [prob_grad_of(*heads[i]) for i in range(4)]
    to_q, to_k, to_v = [], [], []
    for i, (s, pair, h) in enumerate(heads):
        prob_grad = ahead.pop(0)
        if i + 4 < len(heads):
            ahead.append(prob_grad_of(*heads[i + 4]))
        prob_low = prob[s * HEADS + 2 * pair + h]
        prob_full = prob_low.astype(F32)
        weighted = prob_full * prob_grad
        row_dot = jnp.sum(weighted, 0, keepdims=True)
        score_grad = (weighted - prob_full * row_dot).astype(BF16)
        to_v.append(nn(prob_low, go_of(s, pair)))
        k_t = cut(s, pair, 1).T
        to_q.append(nn(k_t[h * HD : (h + 1) * HD], score_grad))
        to_k.append(nn(score_grad, cut(s, pair, 0)))
        if h == 1:
            rows = slice(s * length, (s + 1) * length)
            cols = [slice(c * D + pair * LANES, c * D + (pair + 1) * LANES) for c in range(3)]
            qkv_grad[rows, cols[0]] = (jnp.concatenate(to_q, 0).T * scale).astype(BF16)
            qkv_grad[rows, cols[1]] = (jnp.where(lane < HD, to_k[0], to_k[1]) * scale).astype(BF16)
            qkv_grad[rows, cols[2]] = jnp.where(lane < HD, to_v[0], to_v[1]).astype(BF16)
            to_q, to_k, to_v = [], [], []
    a_t, steps = a()[...].T, None
    for part in range(3):
        cols = slice(part * D, (part + 1) * D)
        piece = nn(a_t, qkv_grad[:, cols])
        for c in range(4):
            flat[pl.ds(ROW_QKV + 4 * part + c, D, stride=12), :] = piece[:, c * LANES : (c + 1) * LANES]
        step = nt(qkv_grad[:, cols], w_qkv()[:, cols])
        steps = step if steps is None else steps + step
    normed[...] = steps
    flat[pl.ds(ROW_GAIN_TWO, rest().shape[0]), :] = rest()[...].astype(F32)
    middle = geo.devices // 2
    early = [d for d in range(middle) if geo.first(d, geo.shard) >= ROW_QKV] if table is None else []
    for d in early:
        chunks.cut(d, flat, 0)
    grad_gain, grad_bias = norm_back(normed, x(), vectors()[0:1, :D], grad_in(), total)
    done(N_GRAD)
    time_grad = [
        jnp.sum(total[s * length : (s + 1) * length, :], 0, keepdims=True).astype(BF16).astype(F32) for s in range(seqs)
    ]
    bias_grad = sum(time_grad[1:], time_grad[0])
    weight_grad = sum(emb_t()[:, s : s + 1] * time_grad[s] for s in range(seqs))
    for c in range(4):
        cols = slice(c * LANES, (c + 1) * LANES)
        flat[pl.ds(ROW_GAIN_ONE + c, 1), :] = grad_gain[:, cols]
        flat[pl.ds(ROW_BIAS_ONE + c, 1), :] = grad_bias[:, cols]
        flat[pl.ds(ROW_B_TIME + c, 1), :] = bias_grad[:, cols]
        flat[pl.ds(ROW_W_TIME + c, TD, stride=4), :] = weight_grad[:, cols]
    if table is not None:
        kind = lax.broadcasted_iota(jnp.int32, (32, tokens), 0)
        table_grad = nn((chars()[...] == kind).astype(BF16), total[...].astype(BF16))
        for c in range(4):
            table[pl.ds(c, 32, stride=4), :] = table_grad[:, c * LANES : (c + 1) * LANES]
    for d in range(middle):
        if d not in early:
            chunks.cut(d, flat, 0, table if chunks.fast else None)
    if table is not None and not chunks.fast:
        for d in range(geo.devices):
            embed_outs[d] = table[pl.ds(geo.first(d, geo.embed_shard), 8), :]


def kept_shapes(seqs, tokens):
    length = tokens // seqs
    return {
        N_X: like(F32, tokens, D),
        N_A: like(BF16, tokens, D),
        N_QKV: like(BF16, tokens, 3 * D),
        N_PROB: like(BF16, seqs * HEADS, length, length),
        N_O: like(BF16, tokens, D),
    }


def rest_rows(geo):
    middle = geo.first(geo.devices // 2, geo.shard)
    return ceil_to(middle + geo.rows - ROW_GAIN_TWO, 16)


def chunk_results(geo, fast):
    if fast:
        shape = like(BF16, geo.devices // 4, geo.rows, LANES)
        return {N_KEEP: shape, N_SEND: shape}
    return {N_KEEP: like(BF16, geo.devices // 2, geo.rows, LANES)}


def chunk_targets(staged, fast):
    return [staged.targets[name] for name in ((N_KEEP, N_SEND) if fast else (N_KEEP,))]


def chunk_scratch(geo, tokens):
    return {
        N_CUTS: pltpu.VMEM((geo.devices // 2, geo.rows, LANES), BF16),
        N_CUT_SEMS: pltpu.SemaphoreType.DMA((geo.devices // 2,)),
        N_NORMED: pltpu.VMEM((tokens, D), F32),
    }


def first_ahead(geo, seqs, place, gathered, chars, emb):
    tokens = chars.shape[0]
    arrays, plan, count = split_gathered(gathered)
    results = WEIGHTS | kept_shapes(seqs, tokens) | {N_X2: like(F32, tokens, D), N_A2: like(BF16, tokens, D)}

    def kernel(place_ref, chunk_refs, staged, extra, sems):
        held = staged.held
        unpack(
            geo, 0, plan, place_ref[0], chunk_refs, extra[N_CHUNKS], extra[N_FLAT], extra[N_FLAT_TABLE], held | extra, sems
        )
        for name in WEIGHTS:
            staged.put(name)
        lane = lax.broadcasted_iota(jnp.int32, (tokens, 32), 1)
        stream = nn((staged.get(N_CHARS)[...] == lane).astype(BF16), extra[N_TABLE][...])
        weights = [extra[N_W_TIME]] + [held[name] for name in (N_W_QKV, N_W_OUT, N_VECTORS)]
        outs = [held[name] for name in (N_X, N_A, N_QKV, N_PROB, N_O, N_X2, N_A2)]
        ahead_attn(seqs, stream, staged.get(N_EMB), *weights, *outs, staged.put)

    operands = {N_CHARS: chars, N_EMB: emb}
    scratch = unpack_scratch(geo, 0)
    return staged_call(kernel, place, operands, results, scratch, 4 * 10**9, arrays, count, parted=())


def first_ahead_rest(place, found):
    names = (N_A2, N_W_UP, N_VECTORS, N_W_DOWN, N_X2)
    operands = {name: found[name] for name in names}
    tokens = found[N_X2].shape[0]
    results = {N_STREAM: like(F32, tokens, D), N_GL: like(BF16, tokens, FF), N_SLOPE: like(BF16, tokens, FF)}

    def kernel(place_ref, _, staged, extra, sems):
        late = [functools.partial(staged.get, name) for name in (N_X2, N_A2, N_W_UP, N_W_DOWN, N_VECTORS)]
        gl, slope, stream = (staged.held[name] for name in (N_GL, N_SLOPE, N_STREAM))
        stream[...] = ahead_mlp(*late, gl, slope, staged.put)
        staged.put(N_STREAM)

    return found | staged_call(kernel, place, operands, results, {}, 4 * 10**9, parted=(N_W_UP, N_W_DOWN, N_GL, N_SLOPE))


def second_both(geo, fast, seqs, place, gathered, stream, emb, cotangent):
    tokens = stream.shape[0]
    arrays, plan, count = split_gathered(gathered)
    results = {name: WEIGHTS[name] for name in (N_W_QKV, N_W_OUT, N_VECTORS)}
    results = results | kept_shapes(seqs, tokens)
    results = results | {
        N_OUTPUT: like(BF16, tokens, D),
        N_GRAD: like(F32, tokens, D),
        N_REST: like(BF16, rest_rows(geo), LANES),
    }
    results = results | chunk_results(geo, fast)
    scratch = unpack_scratch(geo, 1)
    scratch[N_W_UP], scratch[N_W_DOWN] = pltpu.VMEM((D, FF), BF16), pltpu.VMEM((FF, D), BF16)
    scratch[N_X2], scratch[N_A2] = pltpu.VMEM((tokens, D), F32), pltpu.VMEM((tokens, D), BF16)
    scratch[N_GL], scratch[N_SLOPE] = pltpu.VMEM((tokens, FF), BF16), pltpu.VMEM((tokens, FF), BF16)
    scratch = scratch | chunk_scratch(geo, tokens)

    def kernel(place_ref, chunk_arrays, staged, extra, sems):
        every = staged.held | extra
        unpack(geo, 1, plan, place_ref[0], chunk_arrays, extra[N_CHUNKS], extra[N_FLAT], extra[N_FLAT_TABLE], every, sems)
        for name in (N_W_QKV, N_W_OUT, N_VECTORS):
            staged.put(name)
        weights = [every[name] for name in (N_W_TIME, N_W_QKV, N_W_OUT, N_VECTORS)]
        outs = [every[name] for name in (N_X, N_A, N_QKV, N_PROB, N_O, N_X2, N_A2)]

        def done(name, part=None):
            if name in results:
                staged.put(name, part)

        ahead_attn(seqs, staged.get(N_STREAM)[...], staged.get(N_EMB), *weights, *outs, done)

        def ready(*names):
            return [lambda part=None, ref=every[name]: ref for name in names]

        outputs = ahead_mlp(*ready(N_X2, N_A2, N_W_UP, N_W_DOWN, N_VECTORS), every[N_GL], every[N_SLOPE], done)
        every[N_OUTPUT][...] = outputs.astype(BF16)
        done(N_OUTPUT)
        chunks = Chunks(geo, fast, place_ref[0], extra[N_CUTS], chunk_targets(staged, fast), extra[N_CUT_SEMS])
        back_mlp(
            geo, chunks, functools.partial(staged.get, N_COTANGENT),
            *ready(N_X2, N_A2, N_GL, N_SLOPE, N_W_UP, N_W_DOWN, N_VECTORS),
            every[N_GRAD], every[N_REST], extra[N_FLAT], 0, extra[N_NORMED], done,
        )
        chunks.close()

    operands = {N_STREAM: stream, N_EMB: emb, N_COTANGENT: cotangent}
    return staged_call(kernel, place, operands, results, scratch, 10**10, arrays, count, (N_KEEP, N_SEND))


def first_back_mlp(geo, fast, place, grad, found):
    names = (N_GRAD_IN, N_W_DOWN, N_SLOPE, N_GL, N_A2, N_W_UP, N_X2, N_VECTORS)
    operands = {name: grad if name == N_GRAD_IN else found[name] for name in names}
    tokens = grad.shape[0]
    results = {N_GRAD: like(F32, tokens, D), N_REST: like(BF16, rest_rows(geo), LANES)} | chunk_results(geo, fast)
    base = ROW_GAIN_TWO

    def kernel(place_ref, _, staged, extra, sems):
        late = [
            functools.partial(staged.get, name)
            for name in (N_GRAD_IN, N_X2, N_A2, N_GL, N_SLOPE, N_W_UP, N_W_DOWN, N_VECTORS)
        ]
        chunks = Chunks(geo, fast, place_ref[0], extra[N_CUTS], chunk_targets(staged, fast), extra[N_CUT_SEMS])
        back_mlp(
            geo, chunks, *late, staged.held[N_GRAD], staged.held[N_REST], extra[N_FLAT], base, extra[N_NORMED], staged.put
        )
        chunks.close()

    scratch = {N_FLAT: pltpu.VMEM((ROW_END - base + CHUNK_PAD, LANES), F32)} | chunk_scratch(geo, tokens)
    return staged_call(kernel, place, operands, results, scratch, 6 * 10**9, unheld=(N_KEEP, N_SEND))


def both_back_attn(geo, fast, layer, seqs, place, grad, found, emb_t, rest, chars_row):
    names = (N_GRAD_IN, N_W_OUT, N_O, N_QKV, N_PROB, N_A, N_W_QKV, N_X, N_VECTORS, N_EMB_T, N_REST)
    given = {N_GRAD_IN: grad, N_EMB_T: emb_t, N_REST: rest}
    operands = {name: given[name] if name in given else found[name] for name in names}
    tokens = grad.shape[0]
    results = {} if layer == 0 else {N_GRAD: like(F32, tokens, D)}
    results = results | chunk_results(geo, fast)
    scratch = {
        N_FLAT: pltpu.VMEM((ROW_GAIN_TWO + rest.shape[0], LANES), F32),
        N_QKV_GRAD: pltpu.VMEM((tokens, 3 * D), BF16),
        N_HEADS_GRAD: pltpu.VMEM((tokens, D), BF16),
    } | chunk_scratch(geo, tokens)
    if layer == 0:
        scratch[N_TOTAL] = pltpu.VMEM((tokens, D), F32)
        operands[N_CHARS] = chars_row
        scratch[N_TABLE] = pltpu.VMEM((4 * 32, LANES), F32)
        if not fast:
            results[N_TABLE_OUT] = like(F32, geo.devices, 8, LANES)

    def kernel(place_ref, _, staged, extra, sems):
        late = [functools.partial(staged.get, name) for name in (N_GRAD_IN, N_X, N_A, N_QKV, N_PROB, N_O, N_W_QKV, N_W_OUT)]
        tail = [functools.partial(staged.get, name) for name in (N_VECTORS, N_EMB_T, N_REST)]
        chunks = Chunks(geo, fast, place_ref[0], extra[N_CUTS], chunk_targets(staged, fast), extra[N_CUT_SEMS])

        def done(name, part=None):
            if name in results:
                staged.put(name, part)

        back_attn(
            geo, seqs, chunks, extra.get(N_TABLE), staged.held.get(N_TABLE_OUT), *late, *tail,
            extra[N_TOTAL] if layer == 0 else staged.held[N_GRAD], extra[N_FLAT], extra[N_QKV_GRAD], extra[N_HEADS_GRAD],
            extra[N_NORMED], functools.partial(staged.get, N_CHARS), done,
        )
        done(N_TABLE_OUT)
        chunks.close()

    return staged_call(kernel, place, operands, results, scratch, 6 * 10**9, unheld=(N_KEEP, N_SEND))


def permute(value, distance, devices):
    return lax.ppermute(value, AXES, [(d, d ^ distance) for d in range(devices)])


Z1, Z2, Z3, X, Y, CORE = 8, 16, 24, 4, 2, 1


def after(value, *others):
    return lax.optimization_barrier((value, *others))[0]


def sync(*values):
    return lax.optimization_barrier(values)


def gather_both(geo, first, second):
    n, rows = geo.devices, geo.rows
    half = ceil_to(rows // 2, 16)

    def sides(held):
        return permute(held, X, n), permute(held, Y, n)

    def corners(over_x, over_y):
        return permute(over_x[:half], Y, n), permute(over_y[half:], X, n)

    def other(*arrays):
        return permute(jnp.concatenate(arrays, 0), CORE, n)

    near, over = permute(first, Z1, n), permute(first, Z2, n)
    sides_0 = sides(first)
    sides_0 = sync(*sides_0)
    corners_0 = corners(*sides_0)
    near, _ = sync(near, sides_0[0])
    sides_1 = sides(near)
    over, _ = sync(over, near)
    far = permute(over, Z1, n)
    sides_2 = sides(over)
    *sides_1, _ = sync(*sides_1, over)
    corners_1 = corners(*sides_1)
    far, *corners_0 = sync(far, *corners_0, sides_1[0])[:3]
    sides_3 = sides(far)
    other_0 = other(first, *sides_0, *corners_0)
    second, _ = sync(second, far)
    near_b, over_b = permute(second, Z1, n), permute(second, Z2, n)
    *sides_2, _ = sync(*sides_2, far)
    corners_2 = corners(*sides_2)
    *corners_1, _ = sync(*corners_1, sides_2[0])
    other_1 = other(near, *sides_1, *corners_1)
    *sides_3, _ = sync(*sides_3, sides_2[0])
    corners_3 = corners(*sides_3)
    over_b, near_b, _ = sync(over_b, near_b, sides_3[0])
    far_b = permute(over_b, Z1, n)
    *corners_2, _ = sync(*corners_2, sides_3[0])
    other_2 = other(over, *sides_2, *corners_2)
    *corners_3, far_b, _ = sync(*corners_3, far_b, corners_2[0])
    other_3 = other(far, *sides_3, *corners_3)
    column = jnp.concatenate([second, near_b, over_b, far_b], 0)
    found = []
    for z, arrays, packed in (
        (0, (first, *sides_0, *corners_0), other_0),
        (Z1, (near, *sides_1, *corners_1), other_1),
        (Z2, (over, *sides_2, *corners_2), other_2),
        (Z3, (far, *sides_3, *corners_3), other_3),
    ):
        pieces = [
            (0, z, None, 0, rows),
            (rows, z + X, None, 0, rows),
            (2 * rows, z + Y, None, 0, rows),
            (3 * rows, z + X + Y, None, 0, half),
            (3 * rows + half, z + X + Y, None, half, rows - half),
        ]
        for array, (_, relative, _, at, count) in zip(arrays, pieces):
            found.append((array, [(0, relative, None, at, count)]))
        found.append((packed, [(src, rel + CORE, None, at, count) for src, rel, _, at, count in pieces]))
    return found, column


def gather_sides(geo, column):
    return permute(column, X, geo.devices), permute(column, Y, geo.devices)


def gather_corners(geo, over_x, over_y):
    n, rows = geo.devices, geo.rows
    half = ceil_to(rows // 2, 16)
    cut_x = over_x.reshape(4, rows, LANES)[:, :half].reshape(-1, LANES)
    cut_y = over_y.reshape(4, rows, LANES)[:, half:].reshape(-1, LANES)
    return permute(cut_x, Y, n), permute(cut_y, X, n)


def gathered_pieces(geo, arrays, others):
    rows = geo.rows
    half = ceil_to(rows // 2, 16)
    found = []
    for core, group in ((0, arrays), (CORE, others)):
        for array, (relative, at, count) in zip(
            group, ((0, 0, rows), (X, 0, rows), (Y, 0, rows), (X + Y, 0, half), (X + Y, half, rows - half))
        ):
            found.append((array, [(z * count, relative + core + 8 * z, None, at, count) for z in range(4)]))
    return found


def gather_any(geo, chunk):
    gathered = lax.all_gather(chunk, AXES, axis=0)
    return [(gathered, [(0, 0, 0, 0, 0)])]


def add(*values):
    total = values[0].astype(F32)
    for value in values[1:]:
        total = total + value.astype(F32)
    return total


def plane_start(geo, keep, came):
    shape = (2, 2, 2, geo.rows, LANES)
    half = ceil_to(geo.rows // 2, 16)
    keep, came = keep.reshape(shape), came.reshape(shape)
    one = (keep[:, :, :, :half], came[:, :, :, :half])
    two = (keep[:, :, :, half:], came[:, :, :, half:])
    to_x = add(*(part[1] for part in one)).astype(BF16)
    to_y = add(*(part[:, 1] for part in two)).astype(BF16)
    return [part[0] for part in one], [part[:, 0] for part in two], to_x, to_y


def plane_next(one, two, from_x, from_y):
    one, two = one + [from_x], two + [from_y]
    to_y = add(*(part[1] for part in one)).astype(BF16)
    to_x = add(*(part[1] for part in two)).astype(BF16)
    return [part[0] for part in one], [part[0] for part in two], to_y, to_x


def plane_end(one, two, from_y, from_x):
    return jnp.concatenate([add(*one, from_y), add(*two, from_x)], 1)


def column_sum(geo, place, upper, lower, table):
    n = geo.devices
    if table:
        row = lax.broadcasted_iota(jnp.int32, (1, geo.rows, 1), 1)
        upper = jnp.where(row < geo.param_rows, upper, lower)
    is_upper = place[3] >= 2
    near = jnp.where(is_upper, upper, lower)
    far = jnp.where(is_upper, lower, upper).astype(BF16)
    return [near[0], permute(near[1].astype(BF16), Z1, n), permute(far[0], Z2, n), permute(far[1], Z3, n)]


def sum_any(chunks):
    return lax.psum_scatter(chunks.astype(F32), AXES, scatter_dimension=0, tiled=True)[0]


def timestep_embed(step_ids):
    half_dim = TD // 2
    freq_base = jnp.exp(jnp.arange(half_dim, dtype=F32) * (-math.log(10000.0) / half_dim))
    angle_grid = step_ids.astype(F32)[:, None] * freq_base[None, :]
    return jnp.concatenate([jnp.sin(angle_grid), jnp.cos(angle_grid)], axis=1)


def body(fast, chars, steps, embed, layer_params, cotangent):
    seqs, length = chars.shape
    tokens = seqs * length
    geo = Geometry(lax.axis_size(AXES), layer_params.shape[1], embed.shape[0])
    index = lax.axis_index(AXES).astype(jnp.int32)
    place = jnp.stack(
        [index, index * geo.shard % LANES, index * geo.embed_shard % LANES, index // 8]
    ).astype(jnp.int32)
    chunks = pack_shards(geo, place, layer_params, embed)
    emb = timestep_embed(steps).astype(BF16)
    emb_rows = jnp.concatenate([emb, jnp.zeros((8 - seqs, TD), BF16)], 0) if seqs < 8 else emb
    emb_t = emb.astype(F32).T
    chars_row, chars_col = chars.reshape(1, tokens), chars.reshape(tokens, 1)
    n = geo.devices

    cotangent = cotangent.reshape(tokens, D)
    if not fast:
        first = first_ahead(geo, seqs, place, gather_any(geo, chunks[0]), chars_col, emb_rows)
        first = first_ahead_rest(place, first)
        second = second_both(geo, fast, seqs, place, gather_any(geo, chunks[1]), first[N_STREAM], emb_rows, cotangent)
        low_second = both_back_attn(geo, fast, 1, seqs, place, second[N_GRAD], second, emb_t, second[N_REST], chars_row)
        up_first = first_back_mlp(geo, fast, place, low_second[N_GRAD], first)
        low_first = both_back_attn(geo, fast, 0, seqs, place, up_first[N_GRAD], first, emb_t, up_first[N_REST], chars_row)
        sums = [
            sum_any(jnp.concatenate([low_first[N_KEEP], up_first[N_KEEP]], 0)),
            sum_any(jnp.concatenate([low_second[N_KEEP], second[N_KEEP]], 0)),
            sum_any(low_first[N_TABLE_OUT]),
        ]
        grad_params, grad_embed = finish(geo, fast, place, sums)
        return (second[N_OUTPUT].reshape(seqs, length, D), grad_embed, grad_params)

    gathered, column = gather_both(geo, *chunks)
    sides = gather_sides(geo, column)
    column_other = permute(column, CORE, n)
    first = first_ahead(geo, seqs, place, gathered, chars_col, emb_rows)
    first, sides, column_other = sync(first, sides, column_other)
    corners = gather_corners(geo, *sides)
    sides_other = [permute(side, CORE, n) for side in sides]
    first = first_ahead_rest(place, first)
    first, corners, sides_other = sync(first, corners, sides_other)
    corners_other = [permute(corner, CORE, n) for corner in corners]
    pieces = gathered_pieces(geo, [column, *sides, *corners], [column_other, *sides_other, *corners_other])
    second = second_both(geo, fast, seqs, place, pieces, first[N_STREAM], emb_rows, cotangent)
    output = second[N_OUTPUT].reshape(seqs, length, D)

    def cross(to_one, to_two, one, two):
        return permute(to_one, one, n), permute(to_two, two, n)

    def attn(layer, grad, found, rest):
        got = both_back_attn(geo, fast, layer, seqs, place, grad, found, emb_t, rest, chars_row)
        return (got[N_KEEP], got[N_SEND]) if layer == 0 else (got[N_GRAD], got[N_KEEP], got[N_SEND])

    grad, rest, keep_u, send_u = (second[name] for name in (N_GRAD, N_REST, N_KEEP, N_SEND))
    came_u = permute(send_u, CORE, n)
    grad, keep_l, send_l = attn(1, grad, second, rest)
    grad, keep_u, came_u, keep_l, send_l = sync(grad, keep_u, came_u, keep_l, send_l)
    came_l = permute(send_l, CORE, n)
    one_u, two_u, to_x, to_y = plane_start(geo, keep_u, came_u)
    from_u = cross(to_x, to_y, X, Y)

    got = first_back_mlp(geo, fast, place, after(grad, to_x, to_y), first)
    grad, rest, keep, send = (got[name] for name in (N_GRAD, N_REST, N_KEEP, N_SEND))
    grad, rest, keep, send, came_l, from_u = sync(grad, rest, keep, send, came_l, from_u)
    came = permute(send, CORE, n)
    one_u, two_u, to_y, to_x = plane_next(one_u, two_u, *from_u)
    from_u = cross(to_y, to_x, Y, X)
    one_l, two_l, to_x_l, to_y_l = plane_start(geo, keep_l, came_l)
    from_l = cross(to_x_l, to_y_l, X, Y)

    grad = after(grad, to_x, to_y, to_x_l, to_y_l)
    low_keep, low_send = attn(0, grad, first, rest)
    low_keep, low_send, keep, came, from_u, from_l = sync(low_keep, low_send, keep, came, from_u, from_l)
    low_came = permute(low_send, CORE, n)
    one_l, two_l, to_y, to_x = plane_next(one_l, two_l, *from_l)
    from_l = cross(to_y, to_x, Y, X)
    one, two, to_x, to_y = plane_start(geo, keep, came)
    from_up = cross(to_x, to_y, X, Y)
    upper = plane_end(one_u, two_u, *from_u)

    low_came, low_keep, upper, _, _ = sync(low_came, low_keep, upper, to_x, to_y)
    low_one, low_two, to_x, to_y = plane_start(geo, low_keep, low_came)
    from_low = cross(to_x, to_y, X, Y)

    from_l, from_up, _, _ = sync(from_l, from_up, to_x, to_y)
    lower = plane_end(one_l, two_l, *from_l)
    seconds = column_sum(geo, place, upper, lower, False)
    one, two, to_y, to_x = plane_next(one, two, *from_up)
    from_up = cross(to_y, to_x, Y, X)

    from_low, _, _ = sync(from_low, to_y, to_x)
    low_one, low_two, to_y, to_x = plane_next(low_one, low_two, *from_low)
    from_low = cross(to_y, to_x, Y, X)

    from_low, from_up = sync(from_low, from_up)
    upper, lower = plane_end(one, two, *from_up), plane_end(low_one, low_two, *from_low)
    firsts = column_sum(geo, place, upper, lower, True)
    grad_params, grad_embed = finish(geo, fast, place, firsts + seconds)
    return (output, grad_embed, grad_params)


def solution(mesh):
    both = P(AXES)
    fast = dict(mesh.shape) == {"dp": 8, "fsdp": 4}
    return jax.shard_map(
        functools.partial(body, fast),
        mesh=mesh,
        in_specs=(P(AXES, None), both, both, P(None, AXES), P(AXES, None, None)),
        out_specs=(P(AXES, None, None), both, P(None, AXES)),
        check_vma=False,
    )
```

profile of v0, /device:TPU:0, one launch (start us, length us, event | category | flops | bytes accessed | tf_op | source)
XLA Modules:
  0.0 226.5 jit_solution(9025187285522521967)
XLA Ops:
  0.7 1.4 pad_bitcast_fusion
  3.0 3.0 %collective-permute-start.2 = (bf16[800,128]{1,0:T(8,128)(2,1)S(1)}, bf16[800,128]{1,0:T(8,128)(2,1)S(1)}, u32[]{:S(2)}, u32[]{:S(2)}) collective-permute-start(bf16[800,128]{1,0:T(8,128)(2,1)S(1)} %get-tuple-element.137.refs_0_), channel_id=1, source_target_pairs={{0,4},{1,5},{2,6},{3,7},{4,0},{5,1},{6,2},{7,3},{8,12},{9,13},{10,... | collective-permute-start | bytes 614408 | tf_op jit(solution)/shard_map/ppermute | solution.py:800
  6.0 1.5 collective-permute-start.3
  7.5 1.6 collective-permute-start.1
  9.1 2.6 %collective-permute-start = (bf16[800,128]{1,0:T(8,128)(2,1)S(1)}, bf16[800,128]{1,0:T(8,128)(2,1)S(1)}, u32[]{:S(2)}, u32[]{:S(2)}) collective-permute-start(bf16[800,128]{1,0:T(8,128)(2,1)S(1)} %get-tuple-element.137.refs_0_), channel_id=1, source_target_pairs={{0,16},{1,17},{2,18},{3,19},{4,20},{5,21},{6,22},{7,23},{8,24},{9,... | collective-permute-start | bytes 614408 | tf_op jit(solution)/shard_map/ppermute | solution.py:800
  12.6 5.5 %collective-permute-done.1.refs_6_ = bf16[800,128]{1,0:T(8,128)(2,1)S(1)} collective-permute-done((bf16[800,128]{1,0:T(8,128)(2,1)S(1)}, bf16[800,128]{1,0:T(8,128)(2,1)S(1)}, u32[]{:S(2)}, u32[]{:S(2)}) %collective-permute-start.1) | collective-permute-done | bytes 204832 | tf_op jit(solution)/shard_map/ppermute | solution.py:800
  18.9 1.6 collective-permute-done.refs_12_
  22.4 3.6 %collective-permute-done.7.refs_7_ = bf16[800,128]{1,0:T(8,128)(2,1)S(1)} collective-permute-done((bf16[800,128]{1,0:T(8,128)(2,1)S(1)}, bf16[800,128]{1,0:T(8,128)(2,1)S(1)}, u32[]{:S(2)}, u32[]{:S(2)}) %collective-permute-start.7) | collective-permute-done | bytes 204832 | tf_op jit(solution)/shard_map/ppermute | solution.py:800
  26.5 1.4 collective-permute-start.6
  28.0 2.7 %collective-permute-done.5.refs_3_ = bf16[400,128]{1,0:T(8,128)(2,1)S(1)} collective-permute-done((bf16[400,128]{1,0:T(8,128)(2,1)S(1)}, bf16[400,128]{1,0:T(8,128)(2,1)S(1)}, u32[]{:S(2)}, u32[]{:S(2)}) %collective-permute-start.5) | collective-permute-done | bytes 102432 | tf_op jit(solution)/shard_map/ppermute | solution.py:800
  31.8 1.4 collective-permute-start.11
  34.0 1.3 collective-permute-start.18
  36.3 1.9 collective-permute-start.22
  38.3 2.8 %collective-permute-done.21.refs_9_ = bf16[400,128]{1,0:T(8,128)(2,1)S(1)} collective-permute-done((bf16[400,128]{1,0:T(8,128)(2,1)S(1)}, bf16[400,128]{1,0:T(8,128)(2,1)S(1)}, u32[]{:S(2)}, u32[]{:S(2)}) %collective-permute-start.21) | collective-permute-done | bytes 102432 | tf_op jit(solution)/shard_map/ppermute | solution.py:800
  41.8 3.0 %collective-permute-start.9 = (bf16[800,128]{1,0:T(8,128)(2,1)S(1)}, bf16[800,128]{1,0:T(8,128)(2,1)S(1)}, u32[]{:S(2)}, u32[]{:S(2)}) collective-permute-start(bf16[800,128]{1,0:T(8,128)(2,1)S(1)} %get-tuple-element.144), channel_id=1, source_target_pairs={{0,16},{1,17},{2,18},{3,19},{4,20},{5,21},{6,22},{7,23},{8,24},{9,... | collective-permute-start | bytes 614408 | tf_op jit(solution)/shard_map/ppermute | solution.py:800
  45.9 4.8 %collective-permute-done.10 = bf16[800,128]{1,0:T(8,128)(2,1)S(1)} collective-permute-done((bf16[800,128]{1,0:T(8,128)(2,1)S(1)}, bf16[800,128]{1,0:T(8,128)(2,1)S(1)}, u32[]{:S(2)}, u32[]{:S(2)}) %collective-permute-start.10) | collective-permute-done | bytes 204832 | tf_op jit(solution)/shard_map/ppermute | solution.py:800
  50.6 1.5 collective-permute-start.17
  52.2 2.4 %collective-permute-start.15 = (bf16[400,128]{1,0:T(8,128)(2,1)S(1)}, bf16[400,128]{1,0:T(8,128)(2,1)S(1)}, u32[]{:S(2)}, u32[]{:S(2)}) collective-permute-start(bf16[400,128]{1,0:T(8,128)(2,1)S(1)} %slice.381), channel_id=1, source_target_pairs={{0,2},{1,3},{2,0},{3,1},{4,6},{5,7},{6,4},{7,5},{8,10},{9,11},{10,... | collective-permute-start | bytes 307208 | tf_op jit(solution)/shard_map/ppermute | solution.py:800
  54.6 2.6 %collective-permute-done.15.refs_21_ = bf16[400,128]{1,0:T(8,128)(2,1)S(1)} collective-permute-done((bf16[400,128]{1,0:T(8,128)(2,1)S(1)}, bf16[400,128]{1,0:T(8,128)(2,1)S(1)}, u32[]{:S(2)}, u32[]{:S(2)}) %collective-permute-start.15) | collective-permute-done | bytes 102432 | tf_op jit(solution)/shard_map/ppermute | solution.py:800
  57.2 2.0 collective-permute-done.16.refs_22_
  62.6 14.5 %shard_map.77 = (bf16[512,1536]{1,0:T(8,128)(2,1)}, bf16[512,512]{1,0:T(8,128)(2,1)}, bf16[512,2048]{1,0:T(8,128)(2,1)}, bf16[2048,512]{1,0:T(8,128)(2,1)}, f32[...) custom-call(s32[4]{0:T(128)S(1)} %pad_add_fusion.place_ref, ...), custom_call_target="tpu_custom_call" | custom-call | flops 4000000000 | bytes 20000000 | tf_op jit(solution)/shard_map/pallas_call | solution.py:229
  77.1 3.1 %collective-permute-done.26.refs_1_ = bf16[3200,128]{1,0:T(8,128)(2,1)S(1)} collective-permute-done((bf16[3200,128]{1,0:T(8,128)(2,1)S(1)}, bf16[3200,128]{1,0:T(8,128)(2,1)S(1)}, u32[]{:S(2)}, u32[]{:S(2)}) %collective-permute-start.26) | collective-permute-done | bytes 819232 | tf_op jit(solution)/shard_map/ppermute | solution.py:800
  83.0 7.9 %shard_map.78 = (f32[512,512]{1,0:T(8,128)S(1)}, bf16[512,2048]{1,0:T(8,128)(2,1)}, bf16[512,2048]{1,0:T(8,128)(2,1)}) custom-call(s32[4]{0:T(128)S(1)} %pad_add_fusion.place_ref, bf16[512,512]{1,0:T(8,128)(2,1)S(1)} %copy-done.5, bf16[512,2048]{1,0:T(8,128)(2,1)} %get-tuple-element.220.refs_1_.refs_5_, ...), custom_call_target="tpu_custom_call" | custom-call | flops 4000000000 | bytes 20000000 | tf_op jit(solution)/shard_map/pallas_call | solution.py:229
  95.4 24.2 %shard_map.79 = (bf16[512,1536]{1,0:T(8,128)(2,1)}, bf16[512,512]{1,0:T(8,128)(2,1)}, f32[8,2048]{1,0:T(8,128)S(1)}, f32[512,512]{1,0:T(8,128)}, bf16[512,512]{1...) custom-call(s32[4]{0:T(128)S(1)} %pad_add_fusion.place_ref, ...), custom_call_target="tpu_custom_call" | custom-call | flops 10000000000 | bytes 20000000 | tf_op jit(solution)/shard_map/pallas_call | solution.py:229
  123.0 9.8 %shard_map.80 = (f32[512,512]{1,0:T(8,128)}, bf16[8,800,128]{2,1,0:T(8,128)(2,1)}, bf16[8,800,128]{2,1,0:T(8,128)(2,1)}) custom-call(s32[4]{0:T(128)S(1)} %pad_add_fusion.place_ref, f32[512,512]{1,0:T(8,128)} %get-tuple-element.197.refs_0_, bf16[512,512]{1,0:T(8,128)(2,1)S(1)} %copy-done.6, bf16[512,512]{1,0:T(8,128)(2,1)S(1)} %copy-done.8, ...), custom_call_target="tpu_custom_call" | custom-call | flops 6000000000 | bytes 20000000 | tf_op jit(solution)/shard_map/pallas_call | solution.py:229
  133.4 1.3 collective-permute-start.38
  134.9 1.7 collective-permute-start.37
  136.6 11.6 %shard_map.81 = (f32[512,512]{1,0:T(8,128)S(1)}, bf16[4656,128]{1,0:T(8,128)(2,1)}, bf16[8,800,128]{2,1,0:T(8,128)(2,1)}, bf16[8,800,128]{2,1,0:T(8,128)(2,1)}) custom-call(s32[4]{0:T(128)S(1)} %pad_add_fusion.place_ref, f32[512,512]{1,0:T(8,128)} %get-tuple-element.215.refs_0_, bf16[2048,512]{1,0:T(8,128)(2,1)} %get-tuple-element.216.refs_3_.refs_1_, ...), custom_call_target="tpu_custom_call" | custom-call | flops 6000000000 | bytes 20000000 | tf_op jit(solution)/shard_map/pallas_call | solution.py:229
  152.4 1.7 collective-permute-start.41
  154.1 10.6 %shard_map.82 = (bf16[8,800,128]{2,1,0:T(8,128)(2,1)}, bf16[8,800,128]{2,1,0:T(8,128)(2,1)}) custom-call(s32[4]{0:T(128)S(1)} %pad_add_fusion.place_ref, f32[512,512]{1,0:T(8,128)} %copy-done.1, bf16[512,512]{1,0:T(8,128)(2,1)S(1)} %copy-done.2, bf16[512,512]{1,0:T(8,128)(2,1)S(1)} %copy-done.4, bf16[512,1536]{1,0:T(8,128)(2,1)} %get-tuple-element.236.refs_3_, ...), custom_call_target="tpu_custom_call" | custom-call | flops 6000000000 | bytes 20000000 | tf_op jit(solution)/shard_map/pallas_call | solution.py:229
  166.0 1.4 fusion.22
  167.4 1.5 collective-permute-start.44
  172.4 1.6 collective-permute-start.46
  173.9 1.4 fusion.21
  176.6 1.5 collective-permute-start.50
  179.7 4.5 %collective-permute-done.47 = bf16[2,2,400,128]{3,2,1,0:T(8,128)(2,1)S(1)} collective-permute-done((bf16[2,2,400,128]{3,2,1,0:T(8,128)(2,1)S(1)}, bf16[2,2,400,128]{3,2,1,0:T(8,128)(2,1)S(1)}, u32[]{:S(2)}, u32[]{:S(2)}) %collective-permute-start.47) | collective-permute-done | bytes 409632 | tf_op jit(solution)/shard_map/ppermute | solution.py:800
  184.1 1.5 collective-permute-done.46
  185.6 1.5 fusion.11
  192.9 1.5 collective-permute-done.49
  196.2 1.5 collective-permute-start.52
  197.8 2.1 collective-permute-start.60
  199.9 1.5 collective-permute-done.51
  202.4 1.6 fusion.13
  205.2 1.8 collective-permute-start.57
  208.2 5.0 %collective-permute-done.58.refs_5_ = bf16[800,128]{1,0:T(8,128)(2,1)S(1)} collective-permute-done((bf16[800,128]{1,0:T(8,128)(2,1)S(1)}, bf16[800,128]{1,0:T(8,128)(2,1)S(1)}, u32[]{:S(2)}, u32[]{:S(2)}) %collective-permute-start.58) | collective-permute-done | bytes 204832 | tf_op jit(solution)/shard_map/ppermute | solution.py:800
  213.1 8.4 %collective-permute-done.56.refs_2_ = bf16[800,128]{1,0:T(8,128)(2,1)S(1)} collective-permute-done((bf16[800,128]{1,0:T(8,128)(2,1)S(1)}, bf16[800,128]{1,0:T(8,128)(2,1)S(1)}, u32[]{:S(2)}, u32[]{:S(2)}) %collective-permute-start.56) | collective-permute-done | bytes 204832 | tf_op jit(solution)/shard_map/ppermute | solution.py:800
  221.5 1.4 collective-permute-done.55.refs_1_
  223.0 2.7 %shard_map.83 = (f32[2,100512]{1,0:T(2,128)}, f32[8,128]{1,0:T(8,128)S(1)}) custom-call(s32[4]{0:T(128)S(1)} %pad_add_fusion.place_ref, f32[800,128]{1,0:T(8,128)S(1)} %slice_bitcast_fusion.1.refs_0_, bf16[800,128]{1,0:T(8,128)(2,1)S(1)} %collective-permute-done.55.refs_1_, bf16[800,128]{1,0:T(8,128)(2,1)S(1)} %collective-permute-done.56.refs_2_, ...), custom_call_target="tpu_custom_call" | custom-call | flops 1000 | bytes 1000 | tf_op jit(solution)/shard_map/pallas_call | solution.py:146
  (238 shorter events, 47.5 us)
Async XLA Ops:
  3.0 9.6 %collective-permute-start.2 = (bf16[800,128]{1,0:T(8,128)(2,1)S(1)}, bf16[800,128]{1,0:T(8,128)(2,1)S(1)}, u32[]{:S(2)}, u32[]{:S(2)}) collective-permute-start(bf16[800,128]{1,0:T(8,128)(2,1)S(1)} %get-tuple-element.137.refs_0_), channel_id=1, source_target_pairs={{0,4},{1,5},{2,6},{3,7},{4,0},{5,1},{6,2},{7,3},{8,12},{9,13},{10,... | collective-permute-start | bytes 614408 | tf_op jit(solution)/shard_map/ppermute | solution.py:800
  6.0 6.6 %collective-permute-start.3 = (bf16[800,128]{1,0:T(8,128)(2,1)S(1)}, bf16[800,128]{1,0:T(8,128)(2,1)S(1)}, u32[]{:S(2)}, u32[]{:S(2)}) collective-permute-start(bf16[800,128]{1,0:T(8,128)(2,1)S(1)} %get-tuple-element.137.refs_0_), channel_id=1, source_target_pairs={{0,2},{1,3},{2,0},{3,1},{4,6},{5,7},{6,4},{7,5},{8,10},{9,11},{10,... | collective-permute-start | bytes 614408 | tf_op jit(solution)/shard_map/ppermute | solution.py:800
  7.5 10.5 %collective-permute-start.1 = (bf16[800,128]{1,0:T(8,128)(2,1)S(1)}, bf16[800,128]{1,0:T(8,128)(2,1)S(1)}, u32[]{:S(2)}, u32[]{:S(2)}) collective-permute-start(bf16[800,128]{1,0:T(8,128)(2,1)S(1)} %get-tuple-element.137.refs_0_), channel_id=1, source_target_pairs={{0,8},{1,9},{2,10},{3,11},{4,12},{5,13},{6,14},{7,15},{8,0},{9,1},... | collective-permute-start | bytes 614408 | tf_op jit(solution)/shard_map/ppermute | solution.py:800
  9.1 11.4 %collective-permute-start = (bf16[800,128]{1,0:T(8,128)(2,1)S(1)}, bf16[800,128]{1,0:T(8,128)(2,1)S(1)}, u32[]{:S(2)}, u32[]{:S(2)}) collective-permute-start(bf16[800,128]{1,0:T(8,128)(2,1)S(1)} %get-tuple-element.137.refs_0_), channel_id=1, source_target_pairs={{0,16},{1,17},{2,18},{3,19},{4,20},{5,21},{6,22},{7,23},{8,24},{9,... | collective-permute-start | bytes 614408 | tf_op jit(solution)/shard_map/ppermute | solution.py:800
  18.1 8.0 %collective-permute-start.7 = (bf16[800,128]{1,0:T(8,128)(2,1)S(1)}, bf16[800,128]{1,0:T(8,128)(2,1)S(1)}, u32[]{:S(2)}, u32[]{:S(2)}) collective-permute-start(bf16[800,128]{1,0:T(8,128)(2,1)S(1)} %collective-permute-done.1.refs_6_), channel_id=1, source_target_pairs={{0,4},{1,5},{2,6},{3,7},{4,0},{5,1},{6,2},{7,3},{8,12},{9,13},{10,... | collective-permute-start | bytes 614408 | tf_op jit(solution)/shard_map/ppermute | solution.py:800
  18.6 7.9 %collective-permute-start.8 = (bf16[800,128]{1,0:T(8,128)(2,1)S(1)}, bf16[800,128]{1,0:T(8,128)(2,1)S(1)}, u32[]{:S(2)}, u32[]{:S(2)}) collective-permute-start(bf16[800,128]{1,0:T(8,128)(2,1)S(1)} %collective-permute-done.1.refs_6_), channel_id=1, source_target_pairs={{0,2},{1,3},{2,0},{3,1},{4,6},{5,7},{6,4},{7,5},{8,10},{9,11},{10,... | collective-permute-start | bytes 614408 | tf_op jit(solution)/shard_map/ppermute | solution.py:800
  20.5 11.2 %collective-permute-start.4 = (bf16[800,128]{1,0:T(8,128)(2,1)S(1)}, bf16[800,128]{1,0:T(8,128)(2,1)S(1)}, u32[]{:S(2)}, u32[]{:S(2)}) collective-permute-start(bf16[800,128]{1,0:T(8,128)(2,1)S(1)} %collective-permute-done.refs_12_), channel_id=1, source_target_pairs={{0,8},{1,9},{2,10},{3,11},{4,12},{5,13},{6,14},{7,15},{8,0},{9,1},... | collective-permute-start | bytes 614408 | tf_op jit(solution)/shard_map/ppermute | solution.py:800
  20.9 13.1 %collective-permute-start.13 = (bf16[800,128]{1,0:T(8,128)(2,1)S(1)}, bf16[800,128]{1,0:T(8,128)(2,1)S(1)}, u32[]{:S(2)}, u32[]{:S(2)}) collective-permute-start(bf16[800,128]{1,0:T(8,128)(2,1)S(1)} %collective-permute-done.refs_12_), channel_id=1, source_target_pairs={{0,4},{1,5},{2,6},{3,7},{4,0},{5,1},{6,2},{7,3},{8,12},{9,13},{10,... | collective-permute-start | bytes 614408 | tf_op jit(solution)/shard_map/ppermute | solution.py:800
  21.4 12.6 %collective-permute-start.14 = (bf16[800,128]{1,0:T(8,128)(2,1)S(1)}, bf16[800,128]{1,0:T(8,128)(2,1)S(1)}, u32[]{:S(2)}, u32[]{:S(2)}) collective-permute-start(bf16[800,128]{1,0:T(8,128)(2,1)S(1)} %collective-permute-done.refs_12_), channel_id=1, source_target_pairs={{0,2},{1,3},{2,0},{3,1},{4,6},{5,7},{6,4},{7,5},{8,10},{9,11},{10,... | collective-permute-start | bytes 614408 | tf_op jit(solution)/shard_map/ppermute | solution.py:800
  31.8 10.0 %collective-permute-start.11 = (bf16[800,128]{1,0:T(8,128)(2,1)S(1)}, bf16[800,128]{1,0:T(8,128)(2,1)S(1)}, u32[]{:S(2)}, u32[]{:S(2)}) collective-permute-start(bf16[800,128]{1,0:T(8,128)(2,1)S(1)} %collective-permute-done.4.refs_18_), channel_id=1, source_target_pairs={{0,4},{1,5},{2,6},{3,7},{4,0},{5,1},{6,2},{7,3},{8,12},{9,13},{10,... | collective-permute-start | bytes 614408 | tf_op jit(solution)/shard_map/ppermute | solution.py:800
  33.2 11.6 %collective-permute-start.12 = (bf16[800,128]{1,0:T(8,128)(2,1)S(1)}, bf16[800,128]{1,0:T(8,128)(2,1)S(1)}, u32[]{:S(2)}, u32[]{:S(2)}) collective-permute-start(bf16[800,128]{1,0:T(8,128)(2,1)S(1)} %collective-permute-done.4.refs_18_), channel_id=1, source_target_pairs={{0,2},{1,3},{2,0},{3,1},{4,6},{5,7},{6,4},{7,5},{8,10},{9,11},{10,... | collective-permute-start | bytes 614408 | tf_op jit(solution)/shard_map/ppermute | solution.py:800
  34.0 10.9 %collective-permute-start.18 = (bf16[400,128]{1,0:T(8,128)(2,1)S(1)}, bf16[400,128]{1,0:T(8,128)(2,1)S(1)}, u32[]{:S(2)}, u32[]{:S(2)}) collective-permute-start(bf16[400,128]{1,0:T(8,128)(2,1)S(1)} %slice.383), channel_id=1, source_target_pairs={{0,2},{1,3},{2,0},{3,1},{4,6},{5,7},{6,4},{7,5},{8,10},{9,11},{10,... | collective-permute-start | bytes 307208 | tf_op jit(solution)/shard_map/ppermute | solution.py:800
  41.8 8.9 %collective-permute-start.10 = (bf16[800,128]{1,0:T(8,128)(2,1)S(1)}, bf16[800,128]{1,0:T(8,128)(2,1)S(1)}, u32[]{:S(2)}, u32[]{:S(2)}) collective-permute-start(bf16[800,128]{1,0:T(8,128)(2,1)S(1)} %get-tuple-element.144), channel_id=1, source_target_pairs={{0,8},{1,9},{2,10},{3,11},{4,12},{5,13},{6,14},{7,15},{8,0},{9,1},... | collective-permute-start | bytes 614408 | tf_op jit(solution)/shard_map/ppermute | solution.py:800
  41.8 8.8 %collective-permute-start.9 = (bf16[800,128]{1,0:T(8,128)(2,1)S(1)}, bf16[800,128]{1,0:T(8,128)(2,1)S(1)}, u32[]{:S(2)}, u32[]{:S(2)}) collective-permute-start(bf16[800,128]{1,0:T(8,128)(2,1)S(1)} %get-tuple-element.144), channel_id=1, source_target_pairs={{0,16},{1,17},{2,18},{3,19},{4,20},{5,21},{6,22},{7,23},{8,24},{9,... | collective-permute-start | bytes 614408 | tf_op jit(solution)/shard_map/ppermute | solution.py:800
  44.8 14.8 %collective-permute-start.20 = (bf16[3200,128]{1,0:T(8,128)(2,1)S(1)}, bf16[3200,128]{1,0:T(8,128)(2,1)S(1)}, u32[]{:S(2)}, u32[]{:S(2)}) collective-permute-start(bf16[3200,128]{1,0:T(8,128)(2,1)S(1)} %constant_dynamic-update-slice_fusion.4), channel_id=1, source_target_pairs={{0,1},{1,0},{2,3},{3,2},{4,5},{5,4},{6,7},{7,6},{8,9},{9,8},{10,11... | collective-permute-start | bytes 2457608 | tf_op jit(solution)/shard_map/ppermute | solution.py:800
  44.9 15.8 %collective-permute-start.23 = (bf16[3200,128]{1,0:T(8,128)(2,1)S(1)}, bf16[3200,128]{1,0:T(8,128)(2,1)S(1)}, u32[]{:S(2)}, u32[]{:S(2)}) collective-permute-start(bf16[3200,128]{1,0:T(8,128)(2,1)S(1)} %constant_dynamic-update-slice_fusion.9), channel_id=1, source_target_pairs={{0,1},{1,0},{2,3},{3,2},{4,5},{5,4},{6,7},{7,6},{8,9},{9,8},{10,11... | collective-permute-start | bytes 2457608 | tf_op jit(solution)/shard_map/ppermute | solution.py:800
  50.6 8.6 %collective-permute-start.17 = (bf16[800,128]{1,0:T(8,128)(2,1)S(1)}, bf16[800,128]{1,0:T(8,128)(2,1)S(1)}, u32[]{:S(2)}, u32[]{:S(2)}) collective-permute-start(bf16[800,128]{1,0:T(8,128)(2,1)S(1)} %collective-permute-done.9), channel_id=1, source_target_pairs={{0,8},{1,9},{2,10},{3,11},{4,12},{5,13},{6,14},{7,15},{8,0},{9,1},... | collective-permute-start | bytes 614408 | tf_op jit(solution)/shard_map/ppermute | solution.py:800
  59.5 20.7 %collective-permute-start.26 = (bf16[3200,128]{1,0:T(8,128)(2,1)S(1)}, bf16[3200,128]{1,0:T(8,128)(2,1)S(1)}, u32[]{:S(2)}, u32[]{:S(2)}) collective-permute-start(bf16[3200,128]{1,0:T(8,128)(2,1)S(1)} %constant_dynamic-update-slice_fusion.refs_0_), channel_id=1, source_target_pairs={{0,4},{1,5},{2,6},{3,7},{4,0},{5,1},{6,2},{7,3},{8,12},{9,13},{10,... | collective-permute-start | bytes 2457608 | tf_op jit(solution)/shard_map/ppermute | solution.py:800
  59.6 20.7 %collective-permute-start.27 = (bf16[3200,128]{1,0:T(8,128)(2,1)S(1)}, bf16[3200,128]{1,0:T(8,128)(2,1)S(1)}, u32[]{:S(2)}, u32[]{:S(2)}) collective-permute-start(bf16[3200,128]{1,0:T(8,128)(2,1)S(1)} %constant_dynamic-update-slice_fusion.refs_0_), channel_id=1, source_target_pairs={{0,2},{1,3},{2,0},{3,1},{4,6},{5,7},{6,4},{7,5},{8,10},{9,11},{10,... | collective-permute-start | bytes 2457608 | tf_op jit(solution)/shard_map/ppermute | solution.py:800
  60.7 19.6 %collective-permute-start.28 = (bf16[3200,128]{1,0:T(8,128)(2,1)S(1)}, bf16[3200,128]{1,0:T(8,128)(2,1)S(1)}, u32[]{:S(2)}, u32[]{:S(2)}) collective-permute-start(bf16[3200,128]{1,0:T(8,128)(2,1)S(1)} %constant_dynamic-update-slice_fusion.refs_0_), channel_id=1, source_target_pairs={{0,1},{1,0},{2,3},{3,2},{4,5},{5,4},{6,7},{7,6},{8,9},{9,8},{10,11... | collective-permute-start | bytes 2457608 | tf_op jit(solution)/shard_map/ppermute | solution.py:800
  80.3 12.7 %collective-permute-start.31 = (bf16[3200,128]{1,0:T(8,128)(2,1)S(1)}, bf16[3200,128]{1,0:T(8,128)(2,1)S(1)}, u32[]{:S(2)}, u32[]{:S(2)}) collective-permute-start(bf16[3200,128]{1,0:T(8,128)(2,1)S(1)} %collective-permute-done.26.refs_1_), channel_id=1, source_target_pairs={{0,1},{1,0},{2,3},{3,2},{4,5},{5,4},{6,7},{7,6},{8,9},{9,8},{10,11... | collective-permute-start | bytes 2457608 | tf_op jit(solution)/shard_map/ppermute | solution.py:800
  80.4 12.6 %collective-permute-start.32 = (bf16[3200,128]{1,0:T(8,128)(2,1)S(1)}, bf16[3200,128]{1,0:T(8,128)(2,1)S(1)}, u32[]{:S(2)}, u32[]{:S(2)}) collective-permute-start(bf16[3200,128]{1,0:T(8,128)(2,1)S(1)} %collective-permute-done.27.refs_2_), channel_id=1, source_target_pairs={{0,1},{1,0},{2,3},{3,2},{4,5},{5,4},{6,7},{7,6},{8,9},{9,8},{10,11... | collective-permute-start | bytes 2457608 | tf_op jit(solution)/shard_map/ppermute | solution.py:800
  80.9 11.5 %collective-permute-start.29 = (bf16[1600,128]{1,0:T(8,128)(2,1)S(1)}, bf16[1600,128]{1,0:T(8,128)(2,1)S(1)}, u32[]{:S(2)}, u32[]{:S(2)}) collective-permute-start(bf16[1600,128]{1,0:T(8,128)(2,1)S(1)} %bitcast.176), channel_id=1, source_target_pairs={{0,2},{1,3},{2,0},{3,1},{4,6},{5,7},{6,4},{7,5},{8,10},{9,11},{10,... | collective-permute-start | bytes 1228808 | tf_op jit(solution)/shard_map/ppermute | solution.py:800
  81.8 11.2 %collective-permute-start.30 = (bf16[1600,128]{1,0:T(8,128)(2,1)S(1)}, bf16[1600,128]{1,0:T(8,128)(2,1)S(1)}, u32[]{:S(2)}, u32[]{:S(2)}) collective-permute-start(bf16[1600,128]{1,0:T(8,128)(2,1)S(1)} %bitcast.177), channel_id=1, source_target_pairs={{0,4},{1,5},{2,6},{3,7},{4,0},{5,1},{6,2},{7,3},{8,12},{9,13},{10,... | collective-permute-start | bytes 1228808 | tf_op jit(solution)/shard_map/ppermute | solution.py:800
  119.6 13.2 %collective-permute-start.35 = (bf16[8,800,128]{2,1,0:T(8,128)(2,1)}, bf16[8,800,128]{2,1,0:T(8,128)(2,1)S(1)}, u32[]{:S(2)}, u32[]{:S(2)}) collective-permute-start(bf16[8,800,128]{2,1,0:T(8,128)(2,1)} %get-tuple-element.209), channel_id=1, source_target_pairs={{0,1},{1,0},{2,3},{3,2},{4,5},{5,4},{6,7},{7,6},{8,9},{9,8},{10,11... | collective-permute-start | bytes 4915208 | tf_op jit(solution)/shard_map/ppermute | solution.py:800
  132.8 15.4 %collective-permute-start.36 = (bf16[8,800,128]{2,1,0:T(8,128)(2,1)}, bf16[8,800,128]{2,1,0:T(8,128)(2,1)S(1)}, u32[]{:S(2)}, u32[]{:S(2)}) collective-permute-start(bf16[8,800,128]{2,1,0:T(8,128)(2,1)} %get-tuple-element.227), channel_id=1, source_target_pairs={{0,1},{1,0},{2,3},{3,2},{4,5},{5,4},{6,7},{7,6},{8,9},{9,8},{10,11... | collective-permute-start | bytes 4915208 | tf_op jit(solution)/shard_map/ppermute | solution.py:800
  133.4 14.8 %collective-permute-start.38 = (bf16[2,2,400,128]{3,2,1,0:T(8,128)(2,1)S(1)}, bf16[2,2,400,128]{3,2,1,0:T(8,128)(2,1)S(1)}, u32[]{:S(2)}, u32[]{:S(2)}) collective-permute-start(bf16[2,2,400,128]{3,2,1,0:T(8,128)(2,1)S(1)} %fusion.3), channel_id=1, source_target_pairs={{0,2},{1,3},{2,0},{3,1},{4,6},{5,7},{6,4},{7,5},{8,10},{9,11},{10,... | collective-permute-start | bytes 1228808 | tf_op jit(solution)/shard_map/ppermute | solution.py:800
  134.9 13.3 %collective-permute-start.37 = (bf16[2,2,400,128]{3,2,1,0:T(8,128)(2,1)S(1)}, bf16[2,2,400,128]{3,2,1,0:T(8,128)(2,1)S(1)}, u32[]{:S(2)}, u32[]{:S(2)}) collective-permute-start(bf16[2,2,400,128]{3,2,1,0:T(8,128)(2,1)S(1)} %fusion.2), channel_id=1, source_target_pairs={{0,4},{1,5},{2,6},{3,7},{4,0},{5,1},{6,2},{7,3},{8,12},{9,13},{10,... | collective-permute-start | bytes 1228808 | tf_op jit(solution)/shard_map/ppermute | solution.py:800
  148.2 17.7 %collective-permute-start.39 = (bf16[8,800,128]{2,1,0:T(8,128)(2,1)}, bf16[8,800,128]{2,1,0:T(8,128)(2,1)}, u32[]{:S(2)}, u32[]{:S(2)}) collective-permute-start(bf16[8,800,128]{2,1,0:T(8,128)(2,1)} %get-tuple-element.245), channel_id=1, source_target_pairs={{0,1},{1,0},{2,3},{3,2},{4,5},{5,4},{6,7},{7,6},{8,9},{9,8},{10,11... | collective-permute-start | bytes 4915208 | tf_op jit(solution)/shard_map/ppermute | solution.py:800
  148.5 16.8 %collective-permute-start.43 = (bf16[2,2,400,128]{3,2,1,0:T(8,128)(2,1)S(1)}, bf16[2,2,400,128]{3,2,1,0:T(8,128)(2,1)}, u32[]{:S(2)}, u32[]{:S(2)}) collective-permute-start(bf16[2,2,400,128]{3,2,1,0:T(8,128)(2,1)S(1)} %fusion.5), channel_id=1, source_target_pairs={{0,2},{1,3},{2,0},{3,1},{4,6},{5,7},{6,4},{7,5},{8,10},{9,11},{10,... | collective-permute-start | bytes 1228808 | tf_op jit(solution)/shard_map/ppermute | solution.py:800
  149.3 16.0 %collective-permute-start.42 = (bf16[2,2,400,128]{3,2,1,0:T(8,128)(2,1)S(1)}, bf16[2,2,400,128]{3,2,1,0:T(8,128)(2,1)}, u32[]{:S(2)}, u32[]{:S(2)}) collective-permute-start(bf16[2,2,400,128]{3,2,1,0:T(8,128)(2,1)S(1)} %fusion.4), channel_id=1, source_target_pairs={{0,4},{1,5},{2,6},{3,7},{4,0},{5,1},{6,2},{7,3},{8,12},{9,13},{10,... | collective-permute-start | bytes 1228808 | tf_op jit(solution)/shard_map/ppermute | solution.py:800
  151.2 13.6 %collective-permute-start.40 = (bf16[2,400,128]{2,1,0:T(8,128)(2,1)S(1)}, bf16[2,400,128]{2,1,0:T(8,128)(2,1)S(1)}, u32[]{:S(2)}, u32[]{:S(2)}) collective-permute-start(bf16[2,400,128]{2,1,0:T(8,128)(2,1)S(1)} %get-tuple-element.283), channel_id=1, source_target_pairs={{0,2},{1,3},{2,0},{3,1},{4,6},{5,7},{6,4},{7,5},{8,10},{9,11},{10,... | collective-permute-start | bytes 614408 | tf_op jit(solution)/shard_map/ppermute | solution.py:800
  152.4 12.9 %collective-permute-start.41 = (bf16[2,400,128]{2,1,0:T(8,128)(2,1)S(1)}, bf16[2,400,128]{2,1,0:T(8,128)(2,1)S(1)}, u32[]{:S(2)}, u32[]{:S(2)}) collective-permute-start(bf16[2,400,128]{2,1,0:T(8,128)(2,1)S(1)} %get-tuple-element.284), channel_id=1, source_target_pairs={{0,4},{1,5},{2,6},{3,7},{4,0},{5,1},{6,2},{7,3},{8,12},{9,13},{10,... | collective-permute-start | bytes 614408 | tf_op jit(solution)/shard_map/ppermute | solution.py:800
  166.0 9.5 %collective-permute-start.48 = (bf16[8,800,128]{2,1,0:T(8,128)(2,1)}, bf16[8,800,128]{2,1,0:T(8,128)(2,1)}, u32[]{:S(2)}, u32[]{:S(2)}) collective-permute-start(bf16[8,800,128]{2,1,0:T(8,128)(2,1)} %get-tuple-element.250), channel_id=1, source_target_pairs={{0,1},{1,0},{2,3},{3,2},{4,5},{5,4},{6,7},{7,6},{8,9},{9,8},{10,11... | collective-permute-start | bytes 4915208 | tf_op jit(solution)/shard_map/ppermute | solution.py:800
  167.4 11.8 %collective-permute-start.44 = (bf16[2,400,128]{2,1,0:T(8,128)(2,1)S(1)}, bf16[2,400,128]{2,1,0:T(8,128)(2,1)S(1)}, u32[]{:S(2)}, u32[]{:S(2)}) collective-permute-start(bf16[2,400,128]{2,1,0:T(8,128)(2,1)S(1)} %get-tuple-element.280), channel_id=1, source_target_pairs={{0,2},{1,3},{2,0},{3,1},{4,6},{5,7},{6,4},{7,5},{8,10},{9,11},{10,... | collective-permute-start | bytes 614408 | tf_op jit(solution)/shard_map/ppermute | solution.py:800
  168.9 10.8 %collective-permute-start.45 = (bf16[2,400,128]{2,1,0:T(8,128)(2,1)S(1)}, bf16[2,400,128]{2,1,0:T(8,128)(2,1)S(1)}, u32[]{:S(2)}, u32[]{:S(2)}) collective-permute-start(bf16[2,400,128]{2,1,0:T(8,128)(2,1)S(1)} %get-tuple-element.279), channel_id=1, source_target_pairs={{0,4},{1,5},{2,6},{3,7},{4,0},{5,1},{6,2},{7,3},{8,12},{9,13},{10,... | collective-permute-start | bytes 614408 | tf_op jit(solution)/shard_map/ppermute | solution.py:800
  170.4 13.7 %collective-permute-start.47 = (bf16[2,2,400,128]{3,2,1,0:T(8,128)(2,1)S(1)}, bf16[2,2,400,128]{3,2,1,0:T(8,128)(2,1)S(1)}, u32[]{:S(2)}, u32[]{:S(2)}) collective-permute-start(bf16[2,2,400,128]{3,2,1,0:T(8,128)(2,1)S(1)} %fusion.7), channel_id=1, source_target_pairs={{0,2},{1,3},{2,0},{3,1},{4,6},{5,7},{6,4},{7,5},{8,10},{9,11},{10,... | collective-permute-start | bytes 1228808 | tf_op jit(solution)/shard_map/ppermute | solution.py:800
  172.4 13.2 %collective-permute-start.46 = (bf16[2,2,400,128]{3,2,1,0:T(8,128)(2,1)S(1)}, bf16[2,2,400,128]{3,2,1,0:T(8,128)(2,1)S(1)}, u32[]{:S(2)}, u32[]{:S(2)}) collective-permute-start(bf16[2,2,400,128]{3,2,1,0:T(8,128)(2,1)S(1)} %fusion.6), channel_id=1, source_target_pairs={{0,4},{1,5},{2,6},{3,7},{4,0},{5,1},{6,2},{7,3},{8,12},{9,13},{10,... | collective-permute-start | bytes 1228808 | tf_op jit(solution)/shard_map/ppermute | solution.py:800
  176.6 16.3 %collective-permute-start.50 = (bf16[2,2,400,128]{3,2,1,0:T(8,128)(2,1)S(1)}, bf16[2,2,400,128]{3,2,1,0:T(8,128)(2,1)S(1)}, u32[]{:S(2)}, u32[]{:S(2)}) collective-permute-start(bf16[2,2,400,128]{3,2,1,0:T(8,128)(2,1)S(1)} %fusion.9), channel_id=1, source_target_pairs={{0,2},{1,3},{2,0},{3,1},{4,6},{5,7},{6,4},{7,5},{8,10},{9,11},{10,... | collective-permute-start | bytes 1228808 | tf_op jit(solution)/shard_map/ppermute | solution.py:800
  179.2 15.2 %collective-permute-start.49 = (bf16[2,2,400,128]{3,2,1,0:T(8,128)(2,1)S(1)}, bf16[2,2,400,128]{3,2,1,0:T(8,128)(2,1)S(1)}, u32[]{:S(2)}, u32[]{:S(2)}) collective-permute-start(bf16[2,2,400,128]{3,2,1,0:T(8,128)(2,1)S(1)} %fusion.8), channel_id=1, source_target_pairs={{0,4},{1,5},{2,6},{3,7},{4,0},{5,1},{6,2},{7,3},{8,12},{9,13},{10,... | collective-permute-start | bytes 1228808 | tf_op jit(solution)/shard_map/ppermute | solution.py:800
  187.2 19.8 %collective-permute-start.59 = (bf16[800,128]{1,0:T(8,128)(2,1)S(1)}, bf16[800,128]{1,0:T(8,128)(2,1)S(1)}, u32[]{:S(2)}, u32[]{:S(2)}) collective-permute-start(bf16[800,128]{1,0:T(8,128)(2,1)S(1)} %get-tuple-element.286), channel_id=1, source_target_pairs={{0,16},{1,17},{2,18},{3,19},{4,20},{5,21},{6,22},{7,23},{8,24},{9,... | collective-permute-start | bytes 614408 | tf_op jit(solution)/shard_map/ppermute | solution.py:800
  189.3 8.5 %collective-permute-start.53 = (bf16[2,400,128]{2,1,0:T(8,128)(2,1)S(1)}, bf16[2,400,128]{2,1,0:T(8,128)(2,1)S(1)}, u32[]{:S(2)}, u32[]{:S(2)}) collective-permute-start(bf16[2,400,128]{2,1,0:T(8,128)(2,1)S(1)} %get-tuple-element.278), channel_id=1, source_target_pairs={{0,2},{1,3},{2,0},{3,1},{4,6},{5,7},{6,4},{7,5},{8,10},{9,11},{10,... | collective-permute-start | bytes 614408 | tf_op jit(solution)/shard_map/ppermute | solution.py:800
  190.2 9.8 %collective-permute-start.54 = (bf16[2,400,128]{2,1,0:T(8,128)(2,1)S(1)}, bf16[2,400,128]{2,1,0:T(8,128)(2,1)S(1)}, u32[]{:S(2)}, u32[]{:S(2)}) collective-permute-start(bf16[2,400,128]{2,1,0:T(8,128)(2,1)S(1)} %get-tuple-element.277), channel_id=1, source_target_pairs={{0,4},{1,5},{2,6},{3,7},{4,0},{5,1},{6,2},{7,3},{8,12},{9,13},{10,... | collective-permute-start | bytes 614408 | tf_op jit(solution)/shard_map/ppermute | solution.py:800
  197.8 10.3 %collective-permute-start.60 = (bf16[800,128]{1,0:T(8,128)(2,1)S(1)}, bf16[800,128]{1,0:T(8,128)(2,1)S(1)}, u32[]{:S(2)}, u32[]{:S(2)}) collective-permute-start(bf16[800,128]{1,0:T(8,128)(2,1)S(1)} %get-tuple-element.285), channel_id=1, source_target_pairs={{0,24},{1,25},{2,26},{3,27},{4,28},{5,29},{6,30},{7,31},{8,16},{9,... | collective-permute-start | bytes 614408 | tf_op jit(solution)/shard_map/ppermute | solution.py:800
  199.9 13.2 %collective-permute-start.58 = (bf16[800,128]{1,0:T(8,128)(2,1)S(1)}, bf16[800,128]{1,0:T(8,128)(2,1)S(1)}, u32[]{:S(2)}, u32[]{:S(2)}) collective-permute-start(bf16[800,128]{1,0:T(8,128)(2,1)S(1)} %fusion.27), channel_id=1, source_target_pairs={{0,8},{1,9},{2,10},{3,11},{4,12},{5,13},{6,14},{7,15},{8,0},{9,1},... | collective-permute-start | bytes 614408 | tf_op jit(solution)/shard_map/ppermute | solution.py:800
  204.5 17.1 %collective-permute-start.56 = (bf16[800,128]{1,0:T(8,128)(2,1)S(1)}, bf16[800,128]{1,0:T(8,128)(2,1)S(1)}, u32[]{:S(2)}, u32[]{:S(2)}) collective-permute-start(bf16[800,128]{1,0:T(8,128)(2,1)S(1)} %get-tuple-element.288), channel_id=1, source_target_pairs={{0,16},{1,17},{2,18},{3,19},{4,20},{5,21},{6,22},{7,23},{8,24},{9,... | collective-permute-start | bytes 614408 | tf_op jit(solution)/shard_map/ppermute | solution.py:800
  205.2 16.3 %collective-permute-start.57 = (bf16[800,128]{1,0:T(8,128)(2,1)S(1)}, bf16[800,128]{1,0:T(8,128)(2,1)S(1)}, u32[]{:S(2)}, u32[]{:S(2)}) collective-permute-start(bf16[800,128]{1,0:T(8,128)(2,1)S(1)} %get-tuple-element.287), channel_id=1, source_target_pairs={{0,24},{1,25},{2,26},{3,27},{4,28},{5,29},{6,30},{7,31},{8,16},{9,... | collective-permute-start | bytes 614408 | tf_op jit(solution)/shard_map/ppermute | solution.py:800
  207.0 15.9 %collective-permute-start.55 = (bf16[800,128]{1,0:T(8,128)(2,1)S(1)}, bf16[800,128]{1,0:T(8,128)(2,1)S(1)}, u32[]{:S(2)}, u32[]{:S(2)}) collective-permute-start(bf16[800,128]{1,0:T(8,128)(2,1)S(1)} %fusion.26), channel_id=1, source_target_pairs={{0,8},{1,9},{2,10},{3,11},{4,12},{5,13},{6,14},{7,15},{8,0},{9,1},... | collective-permute-start | bytes 614408 | tf_op jit(solution)/shard_map/ppermute | solution.py:800
  (54 other events, 322.6 us)
where the time goes:
time: 231 us; the launch traced here: 227 us
  Pallas kernels  81.9 us (35%)
  waiting for transfers between devices  59.9 us (26%)
  starting transfers between devices  57.1 us (25%)
  other arithmetic  15.3 us (7%)
  local copies, waits for them, and re-layouts  10.4 us (5%)
    pallas_call x6, Pallas kernels, staged_call(): pl.pallas_call(whole, out_shape=tuple(results.values()), in_specs=[SM] +...  78.4 us
    ppermute x61, waiting for transfers between devices, permute(): lax.ppermute(value, AXES, [(d, d ^ distance) for d in range(devices)])  59.9 us
    ppermute x61, starting transfers between devices, permute(): lax.ppermute(value, AXES, [(d, d ^ distance) for d in range(devices)])  57.1 us
    unnamed x105, local copies, waits for them, and re-layouts  8.55 us
  transfers between devices with their start and end apart: 61, of which 28 were waited for; matrix products, arithmetic and copies ran while one was open for 8% of the time, Pallas kernels for 24%

commit v1 on v0

--- a/solution.py
+++ b/solution.py
@@ -151,7 +151,7 @@
         ),
         in_specs=[SM] + [VM] * len(operands),
         out_specs=(VM, VM),
-        scratch_shapes=[pltpu.VMEM((2 * geo.rows, LANES), F32)],
+        scratch_shapes=[pltpu.VMEM((3 * geo.rows, LANES), F32)],
         **params(10**6, geo.rows * 4096),
     )(place, *operands)
     return grads, table.reshape(-1)[: geo.embed_shard]
@@ -314,7 +314,7 @@
     scratch = {
         N_CHUNKS: pltpu.VMEM((geo.devices, geo.rows, LANES), BF16),
         N_FLAT: pltpu.VMEM((ROW_END + CHUNK_PAD, LANES), F32),
-        N_FLAT_TABLE: pltpu.VMEM((4 * 32, LANES), F32),
+        N_FLAT_TABLE: pltpu.VMEM((4 * 34, LANES), F32),
         N_W_TIME: pltpu.VMEM((TD, D), BF16),
     }
     if layer == 0:
@@ -772,7 +772,7 @@
     if layer == 0:
         scratch[N_TOTAL] = pltpu.VMEM((tokens, D), F32)
         operands[N_CHARS] = chars_row
-        scratch[N_TABLE] = pltpu.VMEM((4 * 32, LANES), F32)
+        scratch[N_TABLE] = pltpu.VMEM((4 * 34, LANES), F32)
         if not fast:
             results[N_TABLE_OUT] = like(F32, geo.devices, 8, LANES)
 

time: 231 us -> 231 us (level)
  no operation moved by 1% of the time
where the time goes in v1:
time: 231 us; the launch traced here: 227 us
  Pallas kernels  81.9 us (35%)
  waiting for transfers between devices  59.9 us (26%)
  starting transfers between devices  57.1 us (25%)
  other arithmetic  15.3 us (7%)
  local copies, waits for them, and re-layouts  10.4 us (5%)
    pallas_call x6, Pallas kernels, staged_call(): pl.pallas_call(whole, out_shape=tuple(results.values()), in_specs=[SM] +...  78.4 us
    ppermute x61, waiting for transfers between devices, permute(): lax.ppermute(value, AXES, [(d, d ^ distance) for d in range(devices)])  59.9 us
    ppermute x61, starting transfers between devices, permute(): lax.ppermute(value, AXES, [(d, d ^ distance) for d in range(devices)])  57.1 us
    unnamed x105, local copies, waits for them, and re-layouts  8.55 us
  transfers between devices with their start and end apart: 61, of which 28 were waited for; matrix products, arithmetic and copies ran while one was open for 8% of the time, Pallas kernels for 24%

profile of v1, /device:TPU:0, one launch (start us, length us, event | category | flops | bytes accessed | tf_op | source)
XLA Modules:
  0.0 226.5 jit_solution(8934705588892441897)
XLA Ops:
  0.7 1.4 pad_bitcast_fusion
  3.0 3.0 %collective-permute-start.2 = (bf16[800,128]{1,0:T(8,128)(2,1)S(1)}, bf16[800,128]{1,0:T(8,128)(2,1)S(1)}, u32[]{:S(2)}, u32[]{:S(2)}) collective-permute-start(bf16[800,128]{1,0:T(8,128)(2,1)S(1)} %get-tuple-element.137.refs_0_), channel_id=1, source_target_pairs={{0,4},{1,5},{2,6},{3,7},{4,0},{5,1},{6,2},{7,3},{8,12},{9,13},{10,... | collective-permute-start | bytes 614408 | tf_op jit(solution)/shard_map/ppermute | solution.py:800
  6.0 1.5 collective-permute-start.3
  7.5 1.6 collective-permute-start.1
  9.1 2.6 %collective-permute-start = (bf16[800,128]{1,0:T(8,128)(2,1)S(1)}, bf16[800,128]{1,0:T(8,128)(2,1)S(1)}, u32[]{:S(2)}, u32[]{:S(2)}) collective-permute-start(bf16[800,128]{1,0:T(8,128)(2,1)S(1)} %get-tuple-element.137.refs_0_), channel_id=1, source_target_pairs={{0,16},{1,17},{2,18},{3,19},{4,20},{5,21},{6,22},{7,23},{8,24},{9,... | collective-permute-start | bytes 614408 | tf_op jit(solution)/shard_map/ppermute | solution.py:800
  12.6 5.5 %collective-permute-done.1.refs_6_ = bf16[800,128]{1,0:T(8,128)(2,1)S(1)} collective-permute-done((bf16[800,128]{1,0:T(8,128)(2,1)S(1)}, bf16[800,128]{1,0:T(8,128)(2,1)S(1)}, u32[]{:S(2)}, u32[]{:S(2)}) %collective-permute-start.1) | collective-permute-done | bytes 204832 | tf_op jit(solution)/shard_map/ppermute | solution.py:800
  18.9 1.6 collective-permute-done.refs_12_
  22.4 3.6 %collective-permute-done.7.refs_7_ = bf16[800,128]{1,0:T(8,128)(2,1)S(1)} collective-permute-done((bf16[800,128]{1,0:T(8,128)(2,1)S(1)}, bf16[800,128]{1,0:T(8,128)(2,1)S(1)}, u32[]{:S(2)}, u32[]{:S(2)}) %collective-permute-start.7) | collective-permute-done | bytes 204832 | tf_op jit(solution)/shard_map/ppermute | solution.py:800
  26.5 1.4 collective-permute-start.6
  28.0 2.7 %collective-permute-done.5.refs_3_ = bf16[400,128]{1,0:T(8,128)(2,1)S(1)} collective-permute-done((bf16[400,128]{1,0:T(8,128)(2,1)S(1)}, bf16[400,128]{1,0:T(8,128)(2,1)S(1)}, u32[]{:S(2)}, u32[]{:S(2)}) %collective-permute-start.5) | collective-permute-done | bytes 102432 | tf_op jit(solution)/shard_map/ppermute | solution.py:800
  31.8 1.4 collective-permute-start.11
  34.0 1.3 collective-permute-start.18
  36.3 1.9 collective-permute-start.22
  38.3 2.8 %collective-permute-done.21.refs_9_ = bf16[400,128]{1,0:T(8,128)(2,1)S(1)} collective-permute-done((bf16[400,128]{1,0:T(8,128)(2,1)S(1)}, bf16[400,128]{1,0:T(8,128)(2,1)S(1)}, u32[]{:S(2)}, u32[]{:S(2)}) %collective-permute-start.21) | collective-permute-done | bytes 102432 | tf_op jit(solution)/shard_map/ppermute | solution.py:800
  41.8 3.0 %collective-permute-start.9 = (bf16[800,128]{1,0:T(8,128)(2,1)S(1)}, bf16[800,128]{1,0:T(8,128)(2,1)S(1)}, u32[]{:S(2)}, u32[]{:S(2)}) collective-permute-start(bf16[800,128]{1,0:T(8,128)(2,1)S(1)} %get-tuple-element.144), channel_id=1, source_target_pairs={{0,16},{1,17},{2,18},{3,19},{4,20},{5,21},{6,22},{7,23},{8,24},{9,... | collective-permute-start | bytes 614408 | tf_op jit(solution)/shard_map/ppermute | solution.py:800
  45.9 4.8 %collective-permute-done.10 = bf16[800,128]{1,0:T(8,128)(2,1)S(1)} collective-permute-done((bf16[800,128]{1,0:T(8,128)(2,1)S(1)}, bf16[800,128]{1,0:T(8,128)(2,1)S(1)}, u32[]{:S(2)}, u32[]{:S(2)}) %collective-permute-start.10) | collective-permute-done | bytes 204832 | tf_op jit(solution)/shard_map/ppermute | solution.py:800
  50.6 1.5 collective-permute-start.17
  52.2 2.4 %collective-permute-start.15 = (bf16[400,128]{1,0:T(8,128)(2,1)S(1)}, bf16[400,128]{1,0:T(8,128)(2,1)S(1)}, u32[]{:S(2)}, u32[]{:S(2)}) collective-permute-start(bf16[400,128]{1,0:T(8,128)(2,1)S(1)} %slice.381), channel_id=1, source_target_pairs={{0,2},{1,3},{2,0},{3,1},{4,6},{5,7},{6,4},{7,5},{8,10},{9,11},{10,... | collective-permute-start | bytes 307208 | tf_op jit(solution)/shard_map/ppermute | solution.py:800
  54.6 2.6 %collective-permute-done.15.refs_21_ = bf16[400,128]{1,0:T(8,128)(2,1)S(1)} collective-permute-done((bf16[400,128]{1,0:T(8,128)(2,1)S(1)}, bf16[400,128]{1,0:T(8,128)(2,1)S(1)}, u32[]{:S(2)}, u32[]{:S(2)}) %collective-permute-start.15) | collective-permute-done | bytes 102432 | tf_op jit(solution)/shard_map/ppermute | solution.py:800
  57.2 2.0 collective-permute-done.16.refs_22_
  62.6 14.5 %shard_map.77 = (bf16[512,1536]{1,0:T(8,128)(2,1)}, bf16[512,512]{1,0:T(8,128)(2,1)}, bf16[512,2048]{1,0:T(8,128)(2,1)}, bf16[2048,512]{1,0:T(8,128)(2,1)}, f32[...) custom-call(s32[4]{0:T(128)S(1)} %pad_add_fusion.place_ref, ...), custom_call_target="tpu_custom_call" | custom-call | flops 4000000000 | bytes 20000000 | tf_op jit(solution)/shard_map/pallas_call | solution.py:229
  77.1 3.1 %collective-permute-done.26.refs_1_ = bf16[3200,128]{1,0:T(8,128)(2,1)S(1)} collective-permute-done((bf16[3200,128]{1,0:T(8,128)(2,1)S(1)}, bf16[3200,128]{1,0:T(8,128)(2,1)S(1)}, u32[]{:S(2)}, u32[]{:S(2)}) %collective-permute-start.26) | collective-permute-done | bytes 819232 | tf_op jit(solution)/shard_map/ppermute | solution.py:800
  83.0 7.9 %shard_map.78 = (f32[512,512]{1,0:T(8,128)S(1)}, bf16[512,2048]{1,0:T(8,128)(2,1)}, bf16[512,2048]{1,0:T(8,128)(2,1)}) custom-call(s32[4]{0:T(128)S(1)} %pad_add_fusion.place_ref, bf16[512,512]{1,0:T(8,128)(2,1)S(1)} %copy-done.5, bf16[512,2048]{1,0:T(8,128)(2,1)} %get-tuple-element.220.refs_1_.refs_5_, ...), custom_call_target="tpu_custom_call" | custom-call | flops 4000000000 | bytes 20000000 | tf_op jit(solution)/shard_map/pallas_call | solution.py:229
  95.4 24.2 %shard_map.79 = (bf16[512,1536]{1,0:T(8,128)(2,1)}, bf16[512,512]{1,0:T(8,128)(2,1)}, f32[8,2048]{1,0:T(8,128)S(1)}, f32[512,512]{1,0:T(8,128)}, bf16[512,512]{1...) custom-call(s32[4]{0:T(128)S(1)} %pad_add_fusion.place_ref, ...), custom_call_target="tpu_custom_call" | custom-call | flops 10000000000 | bytes 20000000 | tf_op jit(solution)/shard_map/pallas_call | solution.py:229
  123.0 9.8 %shard_map.80 = (f32[512,512]{1,0:T(8,128)}, bf16[8,800,128]{2,1,0:T(8,128)(2,1)}, bf16[8,800,128]{2,1,0:T(8,128)(2,1)}) custom-call(s32[4]{0:T(128)S(1)} %pad_add_fusion.place_ref, f32[512,512]{1,0:T(8,128)} %get-tuple-element.197.refs_0_, bf16[512,512]{1,0:T(8,128)(2,1)S(1)} %copy-done.6, bf16[512,512]{1,0:T(8,128)(2,1)S(1)} %copy-done.8, ...), custom_call_target="tpu_custom_call" | custom-call | flops 6000000000 | bytes 20000000 | tf_op jit(solution)/shard_map/pallas_call | solution.py:229
  133.4 1.3 collective-permute-start.38
  134.9 1.7 collective-permute-start.37
  136.6 11.6 %shard_map.81 = (f32[512,512]{1,0:T(8,128)S(1)}, bf16[4656,128]{1,0:T(8,128)(2,1)}, bf16[8,800,128]{2,1,0:T(8,128)(2,1)}, bf16[8,800,128]{2,1,0:T(8,128)(2,1)}) custom-call(s32[4]{0:T(128)S(1)} %pad_add_fusion.place_ref, f32[512,512]{1,0:T(8,128)} %get-tuple-element.215.refs_0_, bf16[2048,512]{1,0:T(8,128)(2,1)} %get-tuple-element.216.refs_3_.refs_1_, ...), custom_call_target="tpu_custom_call" | custom-call | flops 6000000000 | bytes 20000000 | tf_op jit(solution)/shard_map/pallas_call | solution.py:229
  152.4 1.7 collective-permute-start.41
  154.1 10.5 %shard_map.82 = (bf16[8,800,128]{2,1,0:T(8,128)(2,1)}, bf16[8,800,128]{2,1,0:T(8,128)(2,1)}) custom-call(s32[4]{0:T(128)S(1)} %pad_add_fusion.place_ref, f32[512,512]{1,0:T(8,128)} %copy-done.1, bf16[512,512]{1,0:T(8,128)(2,1)S(1)} %copy-done.2, bf16[512,512]{1,0:T(8,128)(2,1)S(1)} %copy-done.4, bf16[512,1536]{1,0:T(8,128)(2,1)} %get-tuple-element.236.refs_3_, ...), custom_call_target="tpu_custom_call" | custom-call | flops 6000000000 | bytes 20000000 | tf_op jit(solution)/shard_map/pallas_call | solution.py:229
  166.0 1.4 fusion.22
  167.4 1.5 collective-permute-start.44
  172.4 1.6 collective-permute-start.46
  173.9 1.4 fusion.21
  176.6 1.5 collective-permute-start.50
  179.7 4.5 %collective-permute-done.47 = bf16[2,2,400,128]{3,2,1,0:T(8,128)(2,1)S(1)} collective-permute-done((bf16[2,2,400,128]{3,2,1,0:T(8,128)(2,1)S(1)}, bf16[2,2,400,128]{3,2,1,0:T(8,128)(2,1)S(1)}, u32[]{:S(2)}, u32[]{:S(2)}) %collective-permute-start.47) | collective-permute-done | bytes 409632 | tf_op jit(solution)/shard_map/ppermute | solution.py:800
  184.1 1.5 collective-permute-done.46
  185.6 1.5 fusion.11
  192.9 1.5 collective-permute-done.49
  196.2 1.5 collective-permute-start.52
  197.8 2.1 collective-permute-start.60
  199.9 1.5 collective-permute-done.51
  202.4 1.6 fusion.13
  205.2 1.8 collective-permute-start.57
  208.2 5.0 %collective-permute-done.58.refs_5_ = bf16[800,128]{1,0:T(8,128)(2,1)S(1)} collective-permute-done((bf16[800,128]{1,0:T(8,128)(2,1)S(1)}, bf16[800,128]{1,0:T(8,128)(2,1)S(1)}, u32[]{:S(2)}, u32[]{:S(2)}) %collective-permute-start.58) | collective-permute-done | bytes 204832 | tf_op jit(solution)/shard_map/ppermute | solution.py:800
  213.1 8.4 %collective-permute-done.56.refs_2_ = bf16[800,128]{1,0:T(8,128)(2,1)S(1)} collective-permute-done((bf16[800,128]{1,0:T(8,128)(2,1)S(1)}, bf16[800,128]{1,0:T(8,128)(2,1)S(1)}, u32[]{:S(2)}, u32[]{:S(2)}) %collective-permute-start.56) | collective-permute-done | bytes 204832 | tf_op jit(solution)/shard_map/ppermute | solution.py:800
  221.5 1.4 collective-permute-done.55.refs_1_
  223.0 2.7 %shard_map.83 = (f32[2,100512]{1,0:T(2,128)}, f32[8,128]{1,0:T(8,128)S(1)}) custom-call(s32[4]{0:T(128)S(1)} %pad_add_fusion.place_ref, f32[800,128]{1,0:T(8,128)S(1)} %slice_bitcast_fusion.1.refs_0_, bf16[800,128]{1,0:T(8,128)(2,1)S(1)} %collective-permute-done.55.refs_1_, bf16[800,128]{1,0:T(8,128)(2,1)S(1)} %collective-permute-done.56.refs_2_, ...), custom_call_target="tpu_custom_call" | custom-call | flops 1000 | bytes 1000 | tf_op jit(solution)/shard_map/pallas_call | solution.py:146
  (238 shorter events, 47.5 us)
Async XLA Ops:
  3.0 9.6 %collective-permute-start.2 = (bf16[800,128]{1,0:T(8,128)(2,1)S(1)}, bf16[800,128]{1,0:T(8,128)(2,1)S(1)}, u32[]{:S(2)}, u32[]{:S(2)}) collective-permute-start(bf16[800,128]{1,0:T(8,128)(2,1)S(1)} %get-tuple-element.137.refs_0_), channel_id=1, source_target_pairs={{0,4},{1,5},{2,6},{3,7},{4,0},{5,1},{6,2},{7,3},{8,12},{9,13},{10,... | collective-permute-start | bytes 614408 | tf_op jit(solution)/shard_map/ppermute | solution.py:800
  6.0 6.6 %collective-permute-start.3 = (bf16[800,128]{1,0:T(8,128)(2,1)S(1)}, bf16[800,128]{1,0:T(8,128)(2,1)S(1)}, u32[]{:S(2)}, u32[]{:S(2)}) collective-permute-start(bf16[800,128]{1,0:T(8,128)(2,1)S(1)} %get-tuple-element.137.refs_0_), channel_id=1, source_target_pairs={{0,2},{1,3},{2,0},{3,1},{4,6},{5,7},{6,4},{7,5},{8,10},{9,11},{10,... | collective-permute-start | bytes 614408 | tf_op jit(solution)/shard_map/ppermute | solution.py:800
  7.5 10.5 %collective-permute-start.1 = (bf16[800,128]{1,0:T(8,128)(2,1)S(1)}, bf16[800,128]{1,0:T(8,128)(2,1)S(1)}, u32[]{:S(2)}, u32[]{:S(2)}) collective-permute-start(bf16[800,128]{1,0:T(8,128)(2,1)S(1)} %get-tuple-element.137.refs_0_), channel_id=1, source_target_pairs={{0,8},{1,9},{2,10},{3,11},{4,12},{5,13},{6,14},{7,15},{8,0},{9,1},... | collective-permute-start | bytes 614408 | tf_op jit(solution)/shard_map/ppermute | solution.py:800
  9.1 11.4 %collective-permute-start = (bf16[800,128]{1,0:T(8,128)(2,1)S(1)}, bf16[800,128]{1,0:T(8,128)(2,1)S(1)}, u32[]{:S(2)}, u32[]{:S(2)}) collective-permute-start(bf16[800,128]{1,0:T(8,128)(2,1)S(1)} %get-tuple-element.137.refs_0_), channel_id=1, source_target_pairs={{0,16},{1,17},{2,18},{3,19},{4,20},{5,21},{6,22},{7,23},{8,24},{9,... | collective-permute-start | bytes 614408 | tf_op jit(solution)/shard_map/ppermute | solution.py:800
  18.1 8.0 %collective-permute-start.7 = (bf16[800,128]{1,0:T(8,128)(2,1)S(1)}, bf16[800,128]{1,0:T(8,128)(2,1)S(1)}, u32[]{:S(2)}, u32[]{:S(2)}) collective-permute-start(bf16[800,128]{1,0:T(8,128)(2,1)S(1)} %collective-permute-done.1.refs_6_), channel_id=1, source_target_pairs={{0,4},{1,5},{2,6},{3,7},{4,0},{5,1},{6,2},{7,3},{8,12},{9,13},{10,... | collective-permute-start | bytes 614408 | tf_op jit(solution)/shard_map/ppermute | solution.py:800
  18.6 7.9 %collective-permute-start.8 = (bf16[800,128]{1,0:T(8,128)(2,1)S(1)}, bf16[800,128]{1,0:T(8,128)(2,1)S(1)}, u32[]{:S(2)}, u32[]{:S(2)}) collective-permute-start(bf16[800,128]{1,0:T(8,128)(2,1)S(1)} %collective-permute-done.1.refs_6_), channel_id=1, source_target_pairs={{0,2},{1,3},{2,0},{3,1},{4,6},{5,7},{6,4},{7,5},{8,10},{9,11},{10,... | collective-permute-start | bytes 614408 | tf_op jit(solution)/shard_map/ppermute | solution.py:800
  20.5 11.2 %collective-permute-start.4 = (bf16[800,128]{1,0:T(8,128)(2,1)S(1)}, bf16[800,128]{1,0:T(8,128)(2,1)S(1)}, u32[]{:S(2)}, u32[]{:S(2)}) collective-permute-start(bf16[800,128]{1,0:T(8,128)(2,1)S(1)} %collective-permute-done.refs_12_), channel_id=1, source_target_pairs={{0,8},{1,9},{2,10},{3,11},{4,12},{5,13},{6,14},{7,15},{8,0},{9,1},... | collective-permute-start | bytes 614408 | tf_op jit(solution)/shard_map/ppermute | solution.py:800
  20.9 13.1 %collective-permute-start.13 = (bf16[800,128]{1,0:T(8,128)(2,1)S(1)}, bf16[800,128]{1,0:T(8,128)(2,1)S(1)}, u32[]{:S(2)}, u32[]{:S(2)}) collective-permute-start(bf16[800,128]{1,0:T(8,128)(2,1)S(1)} %collective-permute-done.refs_12_), channel_id=1, source_target_pairs={{0,4},{1,5},{2,6},{3,7},{4,0},{5,1},{6,2},{7,3},{8,12},{9,13},{10,... | collective-permute-start | bytes 614408 | tf_op jit(solution)/shard_map/ppermute | solution.py:800
  21.4 12.6 %collective-permute-start.14 = (bf16[800,128]{1,0:T(8,128)(2,1)S(1)}, bf16[800,128]{1,0:T(8,128)(2,1)S(1)}, u32[]{:S(2)}, u32[]{:S(2)}) collective-permute-start(bf16[800,128]{1,0:T(8,128)(2,1)S(1)} %collective-permute-done.refs_12_), channel_id=1, source_target_pairs={{0,2},{1,3},{2,0},{3,1},{4,6},{5,7},{6,4},{7,5},{8,10},{9,11},{10,... | collective-permute-start | bytes 614408 | tf_op jit(solution)/shard_map/ppermute | solution.py:800
  31.8 10.0 %collective-permute-start.11 = (bf16[800,128]{1,0:T(8,128)(2,1)S(1)}, bf16[800,128]{1,0:T(8,128)(2,1)S(1)}, u32[]{:S(2)}, u32[]{:S(2)}) collective-permute-start(bf16[800,128]{1,0:T(8,128)(2,1)S(1)} %collective-permute-done.4.refs_18_), channel_id=1, source_target_pairs={{0,4},{1,5},{2,6},{3,7},{4,0},{5,1},{6,2},{7,3},{8,12},{9,13},{10,... | collective-permute-start | bytes 614408 | tf_op jit(solution)/shard_map/ppermute | solution.py:800
  33.2 11.6 %collective-permute-start.12 = (bf16[800,128]{1,0:T(8,128)(2,1)S(1)}, bf16[800,128]{1,0:T(8,128)(2,1)S(1)}, u32[]{:S(2)}, u32[]{:S(2)}) collective-permute-start(bf16[800,128]{1,0:T(8,128)(2,1)S(1)} %collective-permute-done.4.refs_18_), channel_id=1, source_target_pairs={{0,2},{1,3},{2,0},{3,1},{4,6},{5,7},{6,4},{7,5},{8,10},{9,11},{10,... | collective-permute-start | bytes 614408 | tf_op jit(solution)/shard_map/ppermute | solution.py:800
  34.0 10.9 %collective-permute-start.18 = (bf16[400,128]{1,0:T(8,128)(2,1)S(1)}, bf16[400,128]{1,0:T(8,128)(2,1)S(1)}, u32[]{:S(2)}, u32[]{:S(2)}) collective-permute-start(bf16[400,128]{1,0:T(8,128)(2,1)S(1)} %slice.383), channel_id=1, source_target_pairs={{0,2},{1,3},{2,0},{3,1},{4,6},{5,7},{6,4},{7,5},{8,10},{9,11},{10,... | collective-permute-start | bytes 307208 | tf_op jit(solution)/shard_map/ppermute | solution.py:800
  41.8 8.9 %collective-permute-start.10 = (bf16[800,128]{1,0:T(8,128)(2,1)S(1)}, bf16[800,128]{1,0:T(8,128)(2,1)S(1)}, u32[]{:S(2)}, u32[]{:S(2)}) collective-permute-start(bf16[800,128]{1,0:T(8,128)(2,1)S(1)} %get-tuple-element.144), channel_id=1, source_target_pairs={{0,8},{1,9},{2,10},{3,11},{4,12},{5,13},{6,14},{7,15},{8,0},{9,1},... | collective-permute-start | bytes 614408 | tf_op jit(solution)/shard_map/ppermute | solution.py:800
  41.8 8.8 %collective-permute-start.9 = (bf16[800,128]{1,0:T(8,128)(2,1)S(1)}, bf16[800,128]{1,0:T(8,128)(2,1)S(1)}, u32[]{:S(2)}, u32[]{:S(2)}) collective-permute-start(bf16[800,128]{1,0:T(8,128)(2,1)S(1)} %get-tuple-element.144), channel_id=1, source_target_pairs={{0,16},{1,17},{2,18},{3,19},{4,20},{5,21},{6,22},{7,23},{8,24},{9,... | collective-permute-start | bytes 614408 | tf_op jit(solution)/shard_map/ppermute | solution.py:800
  44.8 14.8 %collective-permute-start.20 = (bf16[3200,128]{1,0:T(8,128)(2,1)S(1)}, bf16[3200,128]{1,0:T(8,128)(2,1)S(1)}, u32[]{:S(2)}, u32[]{:S(2)}) collective-permute-start(bf16[3200,128]{1,0:T(8,128)(2,1)S(1)} %constant_dynamic-update-slice_fusion.4), channel_id=1, source_target_pairs={{0,1},{1,0},{2,3},{3,2},{4,5},{5,4},{6,7},{7,6},{8,9},{9,8},{10,11... | collective-permute-start | bytes 2457608 | tf_op jit(solution)/shard_map/ppermute | solution.py:800
  44.9 15.8 %collective-permute-start.23 = (bf16[3200,128]{1,0:T(8,128)(2,1)S(1)}, bf16[3200,128]{1,0:T(8,128)(2,1)S(1)}, u32[]{:S(2)}, u32[]{:S(2)}) collective-permute-start(bf16[3200,128]{1,0:T(8,128)(2,1)S(1)} %constant_dynamic-update-slice_fusion.9), channel_id=1, source_target_pairs={{0,1},{1,0},{2,3},{3,2},{4,5},{5,4},{6,7},{7,6},{8,9},{9,8},{10,11... | collective-permute-start | bytes 2457608 | tf_op jit(solution)/shard_map/ppermute | solution.py:800
  50.6 8.6 %collective-permute-start.17 = (bf16[800,128]{1,0:T(8,128)(2,1)S(1)}, bf16[800,128]{1,0:T(8,128)(2,1)S(1)}, u32[]{:S(2)}, u32[]{:S(2)}) collective-permute-start(bf16[800,128]{1,0:T(8,128)(2,1)S(1)} %collective-permute-done.9), channel_id=1, source_target_pairs={{0,8},{1,9},{2,10},{3,11},{4,12},{5,13},{6,14},{7,15},{8,0},{9,1},... | collective-permute-start | bytes 614408 | tf_op jit(solution)/shard_map/ppermute | solution.py:800
  59.5 20.7 %collective-permute-start.26 = (bf16[3200,128]{1,0:T(8,128)(2,1)S(1)}, bf16[3200,128]{1,0:T(8,128)(2,1)S(1)}, u32[]{:S(2)}, u32[]{:S(2)}) collective-permute-start(bf16[3200,128]{1,0:T(8,128)(2,1)S(1)} %constant_dynamic-update-slice_fusion.refs_0_), channel_id=1, source_target_pairs={{0,4},{1,5},{2,6},{3,7},{4,0},{5,1},{6,2},{7,3},{8,12},{9,13},{10,... | collective-permute-start | bytes 2457608 | tf_op jit(solution)/shard_map/ppermute | solution.py:800
  59.6 20.7 %collective-permute-start.27 = (bf16[3200,128]{1,0:T(8,128)(2,1)S(1)}, bf16[3200,128]{1,0:T(8,128)(2,1)S(1)}, u32[]{:S(2)}, u32[]{:S(2)}) collective-permute-start(bf16[3200,128]{1,0:T(8,128)(2,1)S(1)} %constant_dynamic-update-slice_fusion.refs_0_), channel_id=1, source_target_pairs={{0,2},{1,3},{2,0},{3,1},{4,6},{5,7},{6,4},{7,5},{8,10},{9,11},{10,... | collective-permute-start | bytes 2457608 | tf_op jit(solution)/shard_map/ppermute | solution.py:800
  60.7 19.6 %collective-permute-start.28 = (bf16[3200,128]{1,0:T(8,128)(2,1)S(1)}, bf16[3200,128]{1,0:T(8,128)(2,1)S(1)}, u32[]{:S(2)}, u32[]{:S(2)}) collective-permute-start(bf16[3200,128]{1,0:T(8,128)(2,1)S(1)} %constant_dynamic-update-slice_fusion.refs_0_), channel_id=1, source_target_pairs={{0,1},{1,0},{2,3},{3,2},{4,5},{5,4},{6,7},{7,6},{8,9},{9,8},{10,11... | collective-permute-start | bytes 2457608 | tf_op jit(solution)/shard_map/ppermute | solution.py:800
  80.3 12.7 %collective-permute-start.31 = (bf16[3200,128]{1,0:T(8,128)(2,1)S(1)}, bf16[3200,128]{1,0:T(8,128)(2,1)S(1)}, u32[]{:S(2)}, u32[]{:S(2)}) collective-permute-start(bf16[3200,128]{1,0:T(8,128)(2,1)S(1)} %collective-permute-done.26.refs_1_), channel_id=1, source_target_pairs={{0,1},{1,0},{2,3},{3,2},{4,5},{5,4},{6,7},{7,6},{8,9},{9,8},{10,11... | collective-permute-start | bytes 2457608 | tf_op jit(solution)/shard_map/ppermute | solution.py:800
  80.4 12.6 %collective-permute-start.32 = (bf16[3200,128]{1,0:T(8,128)(2,1)S(1)}, bf16[3200,128]{1,0:T(8,128)(2,1)S(1)}, u32[]{:S(2)}, u32[]{:S(2)}) collective-permute-start(bf16[3200,128]{1,0:T(8,128)(2,1)S(1)} %collective-permute-done.27.refs_2_), channel_id=1, source_target_pairs={{0,1},{1,0},{2,3},{3,2},{4,5},{5,4},{6,7},{7,6},{8,9},{9,8},{10,11... | collective-permute-start | bytes 2457608 | tf_op jit(solution)/shard_map/ppermute | solution.py:800
  80.9 11.5 %collective-permute-start.29 = (bf16[1600,128]{1,0:T(8,128)(2,1)S(1)}, bf16[1600,128]{1,0:T(8,128)(2,1)S(1)}, u32[]{:S(2)}, u32[]{:S(2)}) collective-permute-start(bf16[1600,128]{1,0:T(8,128)(2,1)S(1)} %bitcast.176), channel_id=1, source_target_pairs={{0,2},{1,3},{2,0},{3,1},{4,6},{5,7},{6,4},{7,5},{8,10},{9,11},{10,... | collective-permute-start | bytes 1228808 | tf_op jit(solution)/shard_map/ppermute | solution.py:800
  81.8 11.2 %collective-permute-start.30 = (bf16[1600,128]{1,0:T(8,128)(2,1)S(1)}, bf16[1600,128]{1,0:T(8,128)(2,1)S(1)}, u32[]{:S(2)}, u32[]{:S(2)}) collective-permute-start(bf16[1600,128]{1,0:T(8,128)(2,1)S(1)} %bitcast.177), channel_id=1, source_target_pairs={{0,4},{1,5},{2,6},{3,7},{4,0},{5,1},{6,2},{7,3},{8,12},{9,13},{10,... | collective-permute-start | bytes 1228808 | tf_op jit(solution)/shard_map/ppermute | solution.py:800
  119.6 13.2 %collective-permute-start.35 = (bf16[8,800,128]{2,1,0:T(8,128)(2,1)}, bf16[8,800,128]{2,1,0:T(8,128)(2,1)S(1)}, u32[]{:S(2)}, u32[]{:S(2)}) collective-permute-start(bf16[8,800,128]{2,1,0:T(8,128)(2,1)} %get-tuple-element.209), channel_id=1, source_target_pairs={{0,1},{1,0},{2,3},{3,2},{4,5},{5,4},{6,7},{7,6},{8,9},{9,8},{10,11... | collective-permute-start | bytes 4915208 | tf_op jit(solution)/shard_map/ppermute | solution.py:800
  132.8 15.4 %collective-permute-start.36 = (bf16[8,800,128]{2,1,0:T(8,128)(2,1)}, bf16[8,800,128]{2,1,0:T(8,128)(2,1)S(1)}, u32[]{:S(2)}, u32[]{:S(2)}) collective-permute-start(bf16[8,800,128]{2,1,0:T(8,128)(2,1)} %get-tuple-element.227), channel_id=1, source_target_pairs={{0,1},{1,0},{2,3},{3,2},{4,5},{5,4},{6,7},{7,6},{8,9},{9,8},{10,11... | collective-permute-start | bytes 4915208 | tf_op jit(solution)/shard_map/ppermute | solution.py:800
  133.4 14.8 %collective-permute-start.38 = (bf16[2,2,400,128]{3,2,1,0:T(8,128)(2,1)S(1)}, bf16[2,2,400,128]{3,2,1,0:T(8,128)(2,1)S(1)}, u32[]{:S(2)}, u32[]{:S(2)}) collective-permute-start(bf16[2,2,400,128]{3,2,1,0:T(8,128)(2,1)S(1)} %fusion.3), channel_id=1, source_target_pairs={{0,2},{1,3},{2,0},{3,1},{4,6},{5,7},{6,4},{7,5},{8,10},{9,11},{10,... | collective-permute-start | bytes 1228808 | tf_op jit(solution)/shard_map/ppermute | solution.py:800
  134.9 13.3 %collective-permute-start.37 = (bf16[2,2,400,128]{3,2,1,0:T(8,128)(2,1)S(1)}, bf16[2,2,400,128]{3,2,1,0:T(8,128)(2,1)S(1)}, u32[]{:S(2)}, u32[]{:S(2)}) collective-permute-start(bf16[2,2,400,128]{3,2,1,0:T(8,128)(2,1)S(1)} %fusion.2), channel_id=1, source_target_pairs={{0,4},{1,5},{2,6},{3,7},{4,0},{5,1},{6,2},{7,3},{8,12},{9,13},{10,... | collective-permute-start | bytes 1228808 | tf_op jit(solution)/shard_map/ppermute | solution.py:800
  148.2 17.7 %collective-permute-start.39 = (bf16[8,800,128]{2,1,0:T(8,128)(2,1)}, bf16[8,800,128]{2,1,0:T(8,128)(2,1)}, u32[]{:S(2)}, u32[]{:S(2)}) collective-permute-start(bf16[8,800,128]{2,1,0:T(8,128)(2,1)} %get-tuple-element.245), channel_id=1, source_target_pairs={{0,1},{1,0},{2,3},{3,2},{4,5},{5,4},{6,7},{7,6},{8,9},{9,8},{10,11... | collective-permute-start | bytes 4915208 | tf_op jit(solution)/shard_map/ppermute | solution.py:800
  148.5 16.8 %collective-permute-start.43 = (bf16[2,2,400,128]{3,2,1,0:T(8,128)(2,1)S(1)}, bf16[2,2,400,128]{3,2,1,0:T(8,128)(2,1)}, u32[]{:S(2)}, u32[]{:S(2)}) collective-permute-start(bf16[2,2,400,128]{3,2,1,0:T(8,128)(2,1)S(1)} %fusion.5), channel_id=1, source_target_pairs={{0,2},{1,3},{2,0},{3,1},{4,6},{5,7},{6,4},{7,5},{8,10},{9,11},{10,... | collective-permute-start | bytes 1228808 | tf_op jit(solution)/shard_map/ppermute | solution.py:800
  149.3 16.0 %collective-permute-start.42 = (bf16[2,2,400,128]{3,2,1,0:T(8,128)(2,1)S(1)}, bf16[2,2,400,128]{3,2,1,0:T(8,128)(2,1)}, u32[]{:S(2)}, u32[]{:S(2)}) collective-permute-start(bf16[2,2,400,128]{3,2,1,0:T(8,128)(2,1)S(1)} %fusion.4), channel_id=1, source_target_pairs={{0,4},{1,5},{2,6},{3,7},{4,0},{5,1},{6,2},{7,3},{8,12},{9,13},{10,... | collective-permute-start | bytes 1228808 | tf_op jit(solution)/shard_map/ppermute | solution.py:800
  151.2 13.6 %collective-permute-start.40 = (bf16[2,400,128]{2,1,0:T(8,128)(2,1)S(1)}, bf16[2,400,128]{2,1,0:T(8,128)(2,1)S(1)}, u32[]{:S(2)}, u32[]{:S(2)}) collective-permute-start(bf16[2,400,128]{2,1,0:T(8,128)(2,1)S(1)} %get-tuple-element.283), channel_id=1, source_target_pairs={{0,2},{1,3},{2,0},{3,1},{4,6},{5,7},{6,4},{7,5},{8,10},{9,11},{10,... | collective-permute-start | bytes 614408 | tf_op jit(solution)/shard_map/ppermute | solution.py:800
  152.4 12.9 %collective-permute-start.41 = (bf16[2,400,128]{2,1,0:T(8,128)(2,1)S(1)}, bf16[2,400,128]{2,1,0:T(8,128)(2,1)S(1)}, u32[]{:S(2)}, u32[]{:S(2)}) collective-permute-start(bf16[2,400,128]{2,1,0:T(8,128)(2,1)S(1)} %get-tuple-element.284), channel_id=1, source_target_pairs={{0,4},{1,5},{2,6},{3,7},{4,0},{5,1},{6,2},{7,3},{8,12},{9,13},{10,... | collective-permute-start | bytes 614408 | tf_op jit(solution)/shard_map/ppermute | solution.py:800
  166.0 9.5 %collective-permute-start.48 = (bf16[8,800,128]{2,1,0:T(8,128)(2,1)}, bf16[8,800,128]{2,1,0:T(8,128)(2,1)}, u32[]{:S(2)}, u32[]{:S(2)}) collective-permute-start(bf16[8,800,128]{2,1,0:T(8,128)(2,1)} %get-tuple-element.250), channel_id=1, source_target_pairs={{0,1},{1,0},{2,3},{3,2},{4,5},{5,4},{6,7},{7,6},{8,9},{9,8},{10,11... | collective-permute-start | bytes 4915208 | tf_op jit(solution)/shard_map/ppermute | solution.py:800
  167.4 11.8 %collective-permute-start.44 = (bf16[2,400,128]{2,1,0:T(8,128)(2,1)S(1)}, bf16[2,400,128]{2,1,0:T(8,128)(2,1)S(1)}, u32[]{:S(2)}, u32[]{:S(2)}) collective-permute-start(bf16[2,400,128]{2,1,0:T(8,128)(2,1)S(1)} %get-tuple-element.280), channel_id=1, source_target_pairs={{0,2},{1,3},{2,0},{3,1},{4,6},{5,7},{6,4},{7,5},{8,10},{9,11},{10,... | collective-permute-start | bytes 614408 | tf_op jit(solution)/shard_map/ppermute | solution.py:800
  168.9 10.8 %collective-permute-start.45 = (bf16[2,400,128]{2,1,0:T(8,128)(2,1)S(1)}, bf16[2,400,128]{2,1,0:T(8,128)(2,1)S(1)}, u32[]{:S(2)}, u32[]{:S(2)}) collective-permute-start(bf16[2,400,128]{2,1,0:T(8,128)(2,1)S(1)} %get-tuple-element.279), channel_id=1, source_target_pairs={{0,4},{1,5},{2,6},{3,7},{4,0},{5,1},{6,2},{7,3},{8,12},{9,13},{10,... | collective-permute-start | bytes 614408 | tf_op jit(solution)/shard_map/ppermute | solution.py:800
  170.4 13.7 %collective-permute-start.47 = (bf16[2,2,400,128]{3,2,1,0:T(8,128)(2,1)S(1)}, bf16[2,2,400,128]{3,2,1,0:T(8,128)(2,1)S(1)}, u32[]{:S(2)}, u32[]{:S(2)}) collective-permute-start(bf16[2,2,400,128]{3,2,1,0:T(8,128)(2,1)S(1)} %fusion.7), channel_id=1, source_target_pairs={{0,2},{1,3},{2,0},{3,1},{4,6},{5,7},{6,4},{7,5},{8,10},{9,11},{10,... | collective-permute-start | bytes 1228808 | tf_op jit(solution)/shard_map/ppermute | solution.py:800
  172.4 13.2 %collective-permute-start.46 = (bf16[2,2,400,128]{3,2,1,0:T(8,128)(2,1)S(1)}, bf16[2,2,400,128]{3,2,1,0:T(8,128)(2,1)S(1)}, u32[]{:S(2)}, u32[]{:S(2)}) collective-permute-start(bf16[2,2,400,128]{3,2,1,0:T(8,128)(2,1)S(1)} %fusion.6), channel_id=1, source_target_pairs={{0,4},{1,5},{2,6},{3,7},{4,0},{5,1},{6,2},{7,3},{8,12},{9,13},{10,... | collective-permute-start | bytes 1228808 | tf_op jit(solution)/shard_map/ppermute | solution.py:800
  176.6 16.3 %collective-permute-start.50 = (bf16[2,2,400,128]{3,2,1,0:T(8,128)(2,1)S(1)}, bf16[2,2,400,128]{3,2,1,0:T(8,128)(2,1)S(1)}, u32[]{:S(2)}, u32[]{:S(2)}) collective-permute-start(bf16[2,2,400,128]{3,2,1,0:T(8,128)(2,1)S(1)} %fusion.9), channel_id=1, source_target_pairs={{0,2},{1,3},{2,0},{3,1},{4,6},{5,7},{6,4},{7,5},{8,10},{9,11},{10,... | collective-permute-start | bytes 1228808 | tf_op jit(solution)/shard_map/ppermute | solution.py:800
  179.2 15.2 %collective-permute-start.49 = (bf16[2,2,400,128]{3,2,1,0:T(8,128)(2,1)S(1)}, bf16[2,2,400,128]{3,2,1,0:T(8,128)(2,1)S(1)}, u32[]{:S(2)}, u32[]{:S(2)}) collective-permute-start(bf16[2,2,400,128]{3,2,1,0:T(8,128)(2,1)S(1)} %fusion.8), channel_id=1, source_target_pairs={{0,4},{1,5},{2,6},{3,7},{4,0},{5,1},{6,2},{7,3},{8,12},{9,13},{10,... | collective-permute-start | bytes 1228808 | tf_op jit(solution)/shard_map/ppermute | solution.py:800
  187.2 19.8 %collective-permute-start.59 = (bf16[800,128]{1,0:T(8,128)(2,1)S(1)}, bf16[800,128]{1,0:T(8,128)(2,1)S(1)}, u32[]{:S(2)}, u32[]{:S(2)}) collective-permute-start(bf16[800,128]{1,0:T(8,128)(2,1)S(1)} %get-tuple-element.286), channel_id=1, source_target_pairs={{0,16},{1,17},{2,18},{3,19},{4,20},{5,21},{6,22},{7,23},{8,24},{9,... | collective-permute-start | bytes 614408 | tf_op jit(solution)/shard_map/ppermute | solution.py:800
  189.3 8.5 %collective-permute-start.53 = (bf16[2,400,128]{2,1,0:T(8,128)(2,1)S(1)}, bf16[2,400,128]{2,1,0:T(8,128)(2,1)S(1)}, u32[]{:S(2)}, u32[]{:S(2)}) collective-permute-start(bf16[2,400,128]{2,1,0:T(8,128)(2,1)S(1)} %get-tuple-element.278), channel_id=1, source_target_pairs={{0,2},{1,3},{2,0},{3,1},{4,6},{5,7},{6,4},{7,5},{8,10},{9,11},{10,... | collective-permute-start | bytes 614408 | tf_op jit(solution)/shard_map/ppermute | solution.py:800
  190.2 9.8 %collective-permute-start.54 = (bf16[2,400,128]{2,1,0:T(8,128)(2,1)S(1)}, bf16[2,400,128]{2,1,0:T(8,128)(2,1)S(1)}, u32[]{:S(2)}, u32[]{:S(2)}) collective-permute-start(bf16[2,400,128]{2,1,0:T(8,128)(2,1)S(1)} %get-tuple-element.277), channel_id=1, source_target_pairs={{0,4},{1,5},{2,6},{3,7},{4,0},{5,1},{6,2},{7,3},{8,12},{9,13},{10,... | collective-permute-start | bytes 614408 | tf_op jit(solution)/shard_map/ppermute | solution.py:800
  197.8 10.3 %collective-permute-start.60 = (bf16[800,128]{1,0:T(8,128)(2,1)S(1)}, bf16[800,128]{1,0:T(8,128)(2,1)S(1)}, u32[]{:S(2)}, u32[]{:S(2)}) collective-permute-start(bf16[800,128]{1,0:T(8,128)(2,1)S(1)} %get-tuple-element.285), channel_id=1, source_target_pairs={{0,24},{1,25},{2,26},{3,27},{4,28},{5,29},{6,30},{7,31},{8,16},{9,... | collective-permute-start | bytes 614408 | tf_op jit(solution)/shard_map/ppermute | solution.py:800
  199.9 13.2 %collective-permute-start.58 = (bf16[800,128]{1,0:T(8,128)(2,1)S(1)}, bf16[800,128]{1,0:T(8,128)(2,1)S(1)}, u32[]{:S(2)}, u32[]{:S(2)}) collective-permute-start(bf16[800,128]{1,0:T(8,128)(2,1)S(1)} %fusion.27), channel_id=1, source_target_pairs={{0,8},{1,9},{2,10},{3,11},{4,12},{5,13},{6,14},{7,15},{8,0},{9,1},... | collective-permute-start | bytes 614408 | tf_op jit(solution)/shard_map/ppermute | solution.py:800
  204.5 17.1 %collective-permute-start.56 = (bf16[800,128]{1,0:T(8,128)(2,1)S(1)}, bf16[800,128]{1,0:T(8,128)(2,1)S(1)}, u32[]{:S(2)}, u32[]{:S(2)}) collective-permute-start(bf16[800,128]{1,0:T(8,128)(2,1)S(1)} %get-tuple-element.288), channel_id=1, source_target_pairs={{0,16},{1,17},{2,18},{3,19},{4,20},{5,21},{6,22},{7,23},{8,24},{9,... | collective-permute-start | bytes 614408 | tf_op jit(solution)/shard_map/ppermute | solution.py:800
  205.2 16.3 %collective-permute-start.57 = (bf16[800,128]{1,0:T(8,128)(2,1)S(1)}, bf16[800,128]{1,0:T(8,128)(2,1)S(1)}, u32[]{:S(2)}, u32[]{:S(2)}) collective-permute-start(bf16[800,128]{1,0:T(8,128)(2,1)S(1)} %get-tuple-element.287), channel_id=1, source_target_pairs={{0,24},{1,25},{2,26},{3,27},{4,28},{5,29},{6,30},{7,31},{8,16},{9,... | collective-permute-start | bytes 614408 | tf_op jit(solution)/shard_map/ppermute | solution.py:800
  207.0 15.9 %collective-permute-start.55 = (bf16[800,128]{1,0:T(8,128)(2,1)S(1)}, bf16[800,128]{1,0:T(8,128)(2,1)S(1)}, u32[]{:S(2)}, u32[]{:S(2)}) collective-permute-start(bf16[800,128]{1,0:T(8,128)(2,1)S(1)} %fusion.26), channel_id=1, source_target_pairs={{0,8},{1,9},{2,10},{3,11},{4,12},{5,13},{6,14},{7,15},{8,0},{9,1},... | collective-permute-start | bytes 614408 | tf_op jit(solution)/shard_map/ppermute | solution.py:800
  (54 other events, 322.6 us)
